TPU v7x, 128 devices: a whole 4x4x4 slice. The times are simulated.
128 devices in a mesh: mx: 8 (over z_hi, x), my: 16 (over y, z_lo, core).
Axes of the slice: x: 4, y: 4, z: 4 (z_hi: 2, z_lo: 2; z = z_hi * 2 + z_lo), core: 2. Of those that a mesh axis runs over, the one named last changes fastest.
Arguments:
- slab: float32 [192, 192, 6400], P('mx', 'my'), may hold values from -40 to 40
- basis_x: float32 [192, 60], replicated, may hold values from -0.4375 to 0.4375
- basis_y: float32 [192, 60], replicated, may hold values from -0.4375 to 0.4375
Outputs:
- gram_x: float32 [192, 192], replicated
- gram_y: float32 [192, 192], replicated
- core: float32 [60, 60, 6400], P(None, None, ('mx', 'my'))
All inputs are finite; a program needn't handle non-finite values.
Results may differ from a plain program's by a relative error of at most 0.000075.
Values sent between devices are 32-bit elements; how exact they have to be, the bound alone decides.
A program may use at most 192 MiB of HBM per device.

v0:
```python
import jax
import jax.numpy as jnp
from jax import lax
from jax.sharding import PartitionSpec as P

MIDY = 192
RANK = 60
COLS = 6400


def body(slab, basis_x, basis_y):
    high = lax.Precision.HIGHEST
    moved = lax.all_to_all(slab, "mx", split_axis=2, concat_axis=0, tiled=True)
    flat = moved.reshape(moved.shape[0], -1)
    part_x = lax.dot_general(
        flat, flat, (((1,), (1,)), ((), ())), precision=high, preferred_element_type=jnp.float32
    ) / (MIDY * COLS)
    gram_x = lax.psum(part_x, ("mx", "my"))
    first = lax.dot_general(
        basis_x, flat, (((0,), (0,)), ((), ())), precision=high, preferred_element_type=jnp.float32
    )
    first = first.reshape(basis_x.shape[1], moved.shape[1], moved.shape[2])
    second = lax.all_to_all(first, "my", split_axis=2, concat_axis=1, tiled=True)
    batched = lax.dot_general(
        second,
        second,
        (((2,), (2,)), ((0,), (0,))),
        precision=high,
        preferred_element_type=jnp.float32,
    )
    part_y = jnp.sum(batched, axis=0) / (RANK * COLS)
    core = lax.dot_general(
        basis_y,
        second,
        (((0,), (1,)), ((), ())),
        precision=high,
        preferred_element_type=jnp.float32,
    )
    gram_y = lax.psum(part_y, ("mx", "my"))
    return (gram_x, gram_y, core)


def solution(mesh):
    return jax.shard_map(
        body,
        mesh=mesh,
        in_specs=(P("mx", "my", None), P(), P()),
        out_specs=(P(), P(), P(None, None, ("mx", "my"))),
        check_vma=False,
    )
```

profile of v0, /device:TPU:1, one launch (start us, length us, event | category | flops | bytes accessed | tf_op | source)
XLA Modules:
  0.0 629.9 jit_solution(7157276253279038723)
XLA Ops:
  7.2 26.1 %copy.15 = f32[24,12,6400]{0,1,2:T(8,128)} copy(f32[24,12,6400]{2,0,1:T(8,128)} %param.3) | data formatting | bytes 14745600 | tf_op args[0]
  33.3 59.7 %reshape.16 = f32[8,1,230400]{2,1,0:T(1,128)} reshape(f32[6400,12,24]{2,1,0:T(8,128)} %bitcast.31) | data formatting | bytes 14745600
  93.0 93.3 %all_to_all.33 = f32[8,1,230400]{2,1,0:T(1,128)} all-to-all(f32[8,1,230400]{2,1,0:T(1,128)} %reshape.16), channel_id=1, replica_groups=mesh['mx'=8,'my'=16] {'mx'}, dimensions={0} | all-to-all | bytes 14745600 | tf_op jit(solution)/shard_map/all_to_all | solution.py:13
  186.8 80.4 %reduce = f32[8,230400]{1,0:T(8,128)} reduce(f32[8,1,230400]{2,1,0:T(1,128)} %all_to_all.33, f32[]{:T(128)} %broadcast.2), dimensions={1}, to_apply=%all_to_all.24.reduce_sub_computation | reduce | bytes 14745604 | tf_op jit(solution)/shard_map/all_to_all | solution.py:13
  267.1 50.2 %reshape.17 = f32[6400,12,24]{2,1,0:T(8,128)} reshape(f32[8,230400]{1,0:T(8,128)} %reduce) | data formatting | bytes 14745600
  317.3 37.4 %copy.16 = f32[24,12,8,800]{3,1,0,2:T(8,128)} copy(f32[24,12,8,800]{0,1,3,2:T(8,128)} %bitcast.32) | data formatting | bytes 14745600 | tf_op jit(solution)/shard_map/all_to_all | solution.py:13
  354.7 10.5 %reshape.12 = f32[192,9600]{1,0:T(8,128)} reshape(f32[8,24,12,800]{3,2,1,0:T(8,128)} %bitcast.34) | data formatting | bytes 14745600 | tf_op jit(solution)/shard_map/reshape | solution.py:14
  365.2 11.2 %dot_general.20 = f32[12,800,192]{1,0,2:T(8,128)} reshape(f32[9600,192]{0,1:T(8,128)} %bitcast.33) | data formatting | bytes 14745600 | tf_op jit(solution)/shard_map/dot_general | solution.py:19
  376.4 15.8 %fusion = f32[60,12,800]{2,0,1:T(8,128)S(1)} fusion(f32[12,800,192]{1,0,2:T(8,128)} %dot_general.20, f32[192,60]{0,1:T(8,128)S(1)} %copy-done), kind=kOutput, calls=%fused_computation | convolution fusion | flops 1327104000 | bytes 9722880 | tf_op jit(solution)/shard_map/dot_general | solution.py:19
  392.2 5.8 copy.18
  397.9 8.4 %reshape.18 = f32[16,1,36000]{2,1,0:T(1,128)} reshape(f32[800,12,60]{2,1,0:T(8,128)} %bitcast.35) | data formatting | bytes 4608000
  406.3 7.2 %all-to-all-start.1 = ((f32[16,1,36000]{2,1,0:T(1,128)}), f32[16,1,36000]{2,1,0:T(1,128)S(1)}, u32[]{:S(2)}, u32[]{:S(2)}) async-start(f32[16,1,36000]{2,1,0:T(1,128)} %reshape.18), calls=%async_computation.1 | async-start | bytes 4620288 | tf_op jit(solution)/shard_map/all_to_all | solution.py:23
  413.5 10.4 %convolution_multiply_fusion = f32[192,192]{1,0:T(8,128)} fusion(f32[192,9600]{1,0:T(8,128)} %reshape.12), kind=kOutput, calls=%fused_computation.5 | convolution fusion | flops 4246769664 | bytes 7520256 | tf_op jit(solution)/shard_map/dot_general | solution.py:15
  424.0 19.2 %all-to-all-done.1 = f32[16,1,36000]{2,1,0:T(1,128)S(1)} async-done(((f32[16,1,36000]{2,1,0:T(1,128)}), f32[16,1,36000]{2,1,0:T(1,128)S(1)}, u32[]{:S(2)}, u32[]{:S(2)}) %all-to-all-start.1) | async-done | bytes 2304032 | tf_op jit(solution)/shard_map/all_to_all | solution.py:23
  443.2 8.2 %reduce.1 = f32[16,36000]{1,0:T(8,128)} reduce(f32[16,1,36000]{2,1,0:T(1,128)S(1)} %all-to-all-done.1, f32[]{:T(128)} %broadcast.2), dimensions={1}, to_apply=%all_to_all.27.reduce_sub_computation | reduce | bytes 4608004 | tf_op jit(solution)/shard_map/all_to_all | solution.py:23
  451.4 7.3 %reshape.19 = f32[800,12,60]{2,1,0:T(8,128)} reshape(f32[16,36000]{1,0:T(8,128)} %reduce.1) | data formatting | bytes 4608000
  458.7 6.9 %copy.20 = f32[60,16,12,50]{0,3,2,1:T(8,128)} copy(f32[60,16,12,50]{0,2,3,1:T(8,128)} %bitcast.36) | data formatting | bytes 4608000 | tf_op jit(solution)/shard_map/all_to_all | solution.py:23
  465.6 5.5 copy.21
  471.1 6.1 fusion.2
  477.2 3.9 convolution_bitcast_fusion
  481.1 2.8 copy.24
  483.9 135.5 %all-reduce.3.cloned.1.call-done = (f32[192,192]{1,0:T(8,128)}, f32[192,192]{1,0:T(8,128)}) async-done(((f32[192,192]{1,0:T(8,128)}, f32[192,192]{1,0:T(8,128)}), (f32[192,192]{1,0:T(8,128)}, f32[192,192]{1,0:T(8,128)})) %all-reduce.3.cloned.1.call-update) | async-done | bytes 294928 | tf_op jit(solution)/shard_map/psum | solution.py:18
  619.4 1.6 copy.31
  621.0 1.6 copy.32
  (7 shorter events, 0.6 us)
Async XLA Ops:
  7.2 369.2 %copy-start = (f32[192,60]{0,1:T(8,128)S(1)}, f32[192,60]{0,1:T(8,128)}, u32[]{:S(2)}) copy-start(f32[192,60]{0,1:T(8,128)} %param.4) | copy-start | bytes 138244
  406.3 36.9 %all-to-all-start.1 = ((f32[16,1,36000]{2,1,0:T(1,128)}), f32[16,1,36000]{2,1,0:T(1,128)S(1)}, u32[]{:S(2)}, u32[]{:S(2)}) async-start(f32[16,1,36000]{2,1,0:T(1,128)} %reshape.18), calls=%async_computation.1 | async-start | bytes 4620288 | tf_op jit(solution)/shard_map/all_to_all | solution.py:23
  413.5 205.9 %all-reduce.3.cloned.1.call-start = ((), (), s32[]{:S(2)}) async-start(), calls=%async_computation.2 | async-start | bytes 786432 | tf_op jit(solution)/shard_map/psum | solution.py:18
  465.6 11.6 %copy-start.1 = (f32[192,60]{0,1:T(8,128)S(1)}, f32[192,60]{0,1:T(8,128)}, u32[]{:S(2)}) copy-start(f32[192,60]{0,1:T(8,128)} %param.5) | copy-start | bytes 138244
Sparse Core Ops, SparseCore 0:
  477.3 142.0 all-reduce.2
where the time goes:
time: 640 us; the launch traced here: 630 us
  local copies, waits for them, and re-layouts  235 us (37%)
  waiting for transfers between devices  155 us (24%)
  blocking collectives  93.3 us (15%)
  other arithmetic  88.6 us (14%)
  matrix products  36.2 us (6%)
  between operations  14.5 us (2%)
  starting transfers between devices  7.23 us (1%)
    unnamed x12, local copies, waits for them, and re-layouts  158 us
    psum x1, waiting for transfers between devices, body(): gram_x = lax.psum(part_x, ('mx', 'my'))  136 us
    all_to_all x1, blocking collectives, body(): moved = lax.all_to_all(slab, 'mx', split_axis=2, concat_axis=0, tiled=True)  93.3 us
    all_to_all x1, other arithmetic, body(): moved = lax.all_to_all(slab, 'mx', split_axis=2, concat_axis=0, tiled=True)  80.4 us
    all_to_all x2, local copies, waits for them, and re-layouts, body(): moved = lax.all_to_all(slab, 'mx', split_axis=2, concat_axis=0, tiled=True)  37.9 us
    all_to_all x1, waiting for transfers between devices, body(): lax.all_to_all(first, 'my', split_axis=2, concat_axis=1, tiled=True)  19.2 us
    dot_general x2, local copies, waits for them, and re-layouts, body(): lax.dot_general(basis_x, flat, (((0,), (0,)), ((), ())), precision=high,...  17 us
    dot_general x1, matrix products, body(): lax.dot_general(basis_x, flat, (((0,), (0,)), ((), ())), precision=high,...  15.8 us
  transfers between devices with their start and end apart: 2, of which 2 were waited for; matrix products, arithmetic and copies ran while one was open for 3% of the time, Pallas kernels for 0%

commit v1 on v0

v1 whole, which is shorter than its diff:
```python
import functools

import jax
import jax.numpy as jnp
from jax import lax
from jax.experimental import pallas as pl
from jax.experimental.pallas import tpu as pltpu
from jax.sharding import PartitionSpec as P

MESH = pl.DeviceIdType.MESH
F32 = jnp.float32
BF16 = jnp.bfloat16

MIDX = 192
MIDY = 192
RANK = 60
COLS = 6400
JB = 12
IB = 24
OWN = 50
PAIR = 2 * OWN
PACK = 1280
HALF = PACK // 2
HP = OWN // 2
CHUNKS = 4

NT = (((1,), (1,)), ((), ()))
NN = (((1,), (0,)), ((), ()))


def split(a):
    hi = a.astype(BF16)
    return hi, (a - hi.astype(F32)).astype(BF16)


def dot(a, b, dims):
    return lax.dot_general(a, b, dims, preferred_element_type=F32)


def kernel(
    slab, bxt, byt, gx_out, gy_out, core_out,
    raw, s1a, s1b, r1a, r1b, g, ft, fs, fr, bb, bq, gxx, gxm, gyy, gym,
    raw_sem, own_sem, s1_send, s1_recv, s2_send, s2_recv, y_send, y_recv,
):
    mx, my = lax.axis_index("mx"), lax.axis_index("my")
    x, zh = lax.rem(mx, 4), mx // 4
    y, zl, core = my // 4, lax.rem(my // 2, 2), lax.rem(my, 2)
    zz = zl * 2 + zh

    def device(px, py, pz, pc):
        return (lax.rem(pz, 2) * 4 + px, py * 4 + (pz // 2) * 2 + pc)

    def step(v, d):
        return lax.rem(v + d, 4)

    loads = []
    for j in range(JB):
        loads.append(pltpu.make_async_copy(slab.at[j], raw.at[j], raw_sem.at[j]))
        loads[-1].start()

    barrier = pltpu.get_barrier_semaphore()
    partners = [device(step(x, d), y, zz, core) for d in (1, 2, 3)]
    partners += [device(x, y, step(zz, d), core) for d in (1, 2, 3)]
    partners += [device(x, step(y, d), zz, c) for d in (1, 2, 3) for c in (0, 1)]
    partners += [device(x, y, zz, 1 - core)]
    for p in partners:
        pl.semaphore_signal(barrier, inc=1, device_id=p, device_id_type=MESH)

    bb[...] = jnp.zeros_like(bb)
    bb[0:RANK, :] = bxt[...]
    bb[64 : 64 + RANK, :] = bxt[...]
    bq[...] = jnp.zeros_like(bq)
    bq[0:RANK, :] = byt[...]
    for acc in (gxx, gxm, gyy, gym):
        acc[...] = jnp.zeros_like(acc)

    lane = lax.broadcasted_iota(jnp.int32, (IB, 128), 1)

    def pack(k):
        py = step(y, 1 + k)

        def block(b, carry):
            px, pz = b // 4, lax.rem(b, 4)
            off = PAIR * ((lax.rem(pz, 2) * 4 + px) * 8 + py * 2 + pz // 2)
            t0 = off // 128
            t1 = jnp.minimum(t0 + 1, COLS // 128 - 1)
            s = off - t0 * 128
            tiles = [None] * (PACK // 128)
            for j in range(JB):
                d, w = (j * PAIR) % 128, (j * PAIR) // 128
                sh = lax.rem(d - s + 128, 128)
                a = raw[j, :, pl.ds(pl.multiple_of(t0 * 128, 128), 128)]
                c = raw[j, :, pl.ds(pl.multiple_of(t1 * 128, 128), 128)]
                a = pltpu.roll(a, sh, 1)
                c = pltpu.roll(c, sh, 1)
                q = lax.rem(lane - d + 128, 128)
                v = jnp.where(q < 128 - s, a, c)
                tiles[w] = v if tiles[w] is None else jnp.where(lane < d, tiles[w], v)
                if d + PAIR > 128:
                    tiles[w + 1] = v
            tiles[-1] = jnp.where(lane < JB * PAIR - (PACK - 128), tiles[-1], 0.0)
            n = HALF // 128
            for w in range(n):
                s1a[k, px, pz, :, w * 128 : (w + 1) * 128] = tiles[w]
                s1b[k, pz, px, :, w * 128 : (w + 1) * 128] = tiles[n + w]
            return carry

        lax.fori_loop(0, 16, block, 0)

    def remote(src, dst, ssem, rsem, dev):
        return pltpu.make_async_remote_copy(
            src_ref=src, dst_ref=dst, send_sem=ssem, recv_sem=rsem, device_id=dev, device_id_type=MESH
        )

    def first_hop(k):
        out = []
        for d in (2, 1, 3):
            px, pz = step(x, d), step(zz, d)
            out.append(remote(s1a.at[k, px], r1a.at[k, x], s1_send.at[k, 0, d - 1], s1_recv.at[k, 0, d - 1], device(px, y, zz, core)))
            out.append(remote(s1b.at[k, pz], r1b.at[k, zz], s1_send.at[k, 1, d - 1], s1_recv.at[k, 1, d - 1], device(x, y, pz, core)))
        own = [
            pltpu.make_async_copy(s1a.at[k, x], r1a.at[k, x], own_sem.at[k, 0]),
            pltpu.make_async_copy(s1b.at[k, zz], r1b.at[k, zz], own_sem.at[k, 1]),
        ]
        for c in out + own:
            c.start()
        return out, own

    def second_hop(k):
        out = []
        for d in (2, 1, 3):
            px, pz = step(x, d), step(zz, d)
            out.append(remote(r1a.at[k, :, pz], g.at[k, 0, zz], s2_send.at[k, 0, d - 1], s2_recv.at[k, 0, d - 1], device(x, y, pz, core)))
            out.append(remote(r1b.at[k, :, px], g.at[k, 1, :, x], s2_send.at[k, 1, d - 1], s2_recv.at[k, 1, d - 1], device(px, y, zz, core)))
        own = [
            pltpu.make_async_copy(r1a.at[k, :, zz], g.at[k, 0, zz], own_sem.at[k, 2]),
            pltpu.make_async_copy(r1b.at[k, :, x], g.at[k, 1, :, x], own_sem.at[k, 3]),
        ]
        for c in out + own:
            c.start()
        return out, own

    def arrive(hop):
        out, own = hop
        for c in out:
            c.wait_recv()
        for c in own:
            c.wait()

    low = lax.broadcasted_iota(jnp.int32, (JB, 128), 1) < 64

    def project(k):
        def block(u, carry):
            h, v = u // 2, lax.rem(u, 2)
            a = g[k, h, pl.ds(v * 2, 2)].reshape(MIDX, HALF)
            hi, lo = split(a)
            gxx[...] += dot(hi, hi, NT)
            gxm[...] += dot(hi, lo, NT)
            bhi, blo = split(bb[...])
            f = dot(bhi, hi, NN) + (dot(blo, hi, NN) + dot(bhi, lo, NN))
            ft[v, pl.ds(pl.multiple_of(h * HALF, HALF), HALF), :] = f.T
            return carry

        lax.fori_loop(0, 4, block, 0)

        def pairs(p, carry):
            for c in (0, 1):
                for v in (0, 1):
                    a = ft[v, pl.ds(c * OWN + p, JB, PAIR), :]
                    b = ft[v, pl.ds(c * OWN + HP + p, JB, PAIR), :]
                    fs[k, c, p, v * JB : (v + 1) * JB, :] = jnp.where(low, a, b)
            return carry

        lax.fori_loop(0, HP, pairs, 0)

    def spread(k):
        py = step(y, 1 + k)
        if k < CHUNKS - 1:
            out = [
                remote(fs.at[k, c], fr.at[y, core], y_send.at[k, c], y_recv.at[k, core], device(x, py, zz, c))
                for c in (0, 1)
            ]
            own = []
        else:
            c = 1 - core
            out = [remote(fs.at[k, c], fr.at[y, core], y_send.at[k, 0], y_recv.at[k, core], device(x, y, zz, c))]
            own = [pltpu.make_async_copy(fs.at[k, core], fr.at[y, core], y_send.at[k, 1])]
        for c in out + own:
            c.start()
        return out, own

    for c in loads:
        c.wait()
    pack(0)
    pl.semaphore_wait(barrier, len(partners))
    hops1, hops2, hops3 = [first_hop(0)], [], []
    pack(1)
    hops1.append(first_hop(1))
    for k in range(CHUNKS):
        arrive(hops1[k])
        hops2.append(second_hop(k))
        if k + 2 < CHUNKS:
            pack(k + 2)
            hops1.append(first_hop(k + 2))
        if k > 0:
            arrive(hops2[k - 1])
            project(k - 1)
            hops3.append(spread(k - 1))
    arrive(hops2[-1])
    project(CHUNKS - 1)
    hops3.append(spread(CHUNKS - 1))

    for k in range(CHUNKS - 1):
        for c in (0, 1):
            remote(fs.at[k, c], fr.at[step(y, 3 - k), c], y_send.at[k, c], y_recv.at[k, c], device(x, y, zz, c)).wait_recv()
    out, own = hops3[-1]
    remote(fs.at[CHUNKS - 1, core], fr.at[y, 1 - core], y_send.at[CHUNKS - 1, 0], y_recv.at[CHUNKS - 1, 1 - core], device(x, y, zz, 1 - core)).wait_recv()
    own[0].wait()

    qhi, qlo = split(bq[...])
    wide = 5

    def finish(u, carry):
        parts = []
        for e in range(wide):
            p = u * wide + e
            rows = []
            for s in range(4):
                a, b = fr[s, 0, p], fr[s, 1, p]
                rows += [a[:JB], b[:JB], a[JB:], b[JB:]]
            parts.append(jnp.concatenate(rows, axis=0))
        hi, lo = split(jnp.concatenate(parts, axis=1))
        gyy[...] += dot(hi, hi, NT)
        gym[...] += dot(hi, lo, NT)
        c = dot(qhi, hi, NN) + (dot(qlo, hi, NN) + dot(qhi, lo, NN))
        for e in range(wide):
            p = u * wide + e
            v = c[:, e * 128 : (e + 1) * 128]
            core_out[p] = v[:RANK, :RANK]
            core_out[p + HP] = pltpu.roll(v, 64, 1)[:RANK, :RANK]
        return carry

    lax.fori_loop(0, HP // wide, finish, 0)
    gx_out[...] = (gxx[...] + (gxm[...] + gxm[...].T)) * (1.0 / (MIDY * COLS))
    gy_out[...] = (gyy[...] + (gym[...] + gym[...].T)) * (1.0 / (RANK * COLS))

    for out, _ in hops1 + hops2 + hops3:
        for c in out:
            c.wait_send()


def body(slab, basis_x, basis_y):
    vmem = pl.BlockSpec(memory_space=pltpu.VMEM)
    gx, gy, core = pl.pallas_call(
        kernel,
        out_shape=(
            jax.ShapeDtypeStruct((MIDX, MIDX), F32),
            jax.ShapeDtypeStruct((MIDY, MIDY), F32),
            jax.ShapeDtypeStruct((OWN, RANK, RANK), F32),
        ),
        in_specs=[pl.BlockSpec(memory_space=pl.ANY), vmem, vmem],
        out_specs=(vmem, vmem, vmem),
        scratch_shapes=[
            pltpu.VMEM((JB, IB, COLS), F32),
            pltpu.VMEM((CHUNKS, 4, 4, IB, HALF), F32),
            pltpu.VMEM((CHUNKS, 4, 4, IB, HALF), F32),
            pltpu.VMEM((CHUNKS, 4, 4, IB, HALF), F32),
            pltpu.VMEM((CHUNKS, 4, 4, IB, HALF), F32),
            pltpu.VMEM((CHUNKS, 2, 4, 4, IB, HALF), F32),
            pltpu.VMEM((2, PACK, 128), F32),
            pltpu.VMEM((CHUNKS, 2, HP, 2 * JB, 128), F32),
            pltpu.VMEM((4, 2, HP, 2 * JB, 128), F32),
            pltpu.VMEM((128, MIDX), F32),
            pltpu.VMEM((64, MIDY), F32),
            pltpu.VMEM((MIDX, MIDX), F32),
            pltpu.VMEM((MIDX, MIDX), F32),
            pltpu.VMEM((MIDY, MIDY), F32),
            pltpu.VMEM((MIDY, MIDY), F32),
            pltpu.SemaphoreType.DMA((JB,)),
            pltpu.SemaphoreType.DMA((CHUNKS, 4)),
            pltpu.SemaphoreType.DMA((CHUNKS, 2, 3)),
            pltpu.SemaphoreType.DMA((CHUNKS, 2, 3)),
            pltpu.SemaphoreType.DMA((CHUNKS, 2, 3)),
            pltpu.SemaphoreType.DMA((CHUNKS, 2, 3)),
            pltpu.SemaphoreType.DMA((CHUNKS, 2)),
            pltpu.SemaphoreType.DMA((CHUNKS, 2)),
        ],
        compiler_params=pltpu.CompilerParams(
            collective_id=0, has_side_effects=True, vmem_limit_bytes=58 * 2**20
        ),
    )(jnp.transpose(slab, (1, 0, 2)), basis_x.T, basis_y.T)
    gx, gy = lax.psum((gx, gy), ("mx", "my"))
    return gx, gy, jnp.transpose(core, (1, 2, 0))


def solution(mesh):
    return jax.shard_map(
        body,
        mesh=mesh,
        in_specs=(P("mx", "my", None), P(), P()),
        out_specs=(P(), P(), P(None, None, ("mx", "my"))),
        check_vma=False,
    )
```

time: 640 us -> 273 us (0.43); the launches traced: 630 us -> 273 us
  local copies, waits for them, and re-layouts: 235 us -> 6.01 us
  Pallas kernels: 0 us -> 109 us
  blocking collectives: 93.3 us -> 0 us
  other arithmetic: 88.6 us -> 0 us
  matrix products: 36.2 us -> 0 us
  waiting for transfers between devices: 155 us -> 144 us
  starting transfers between devices: 7.23 us -> 0.04 us
    unnamed x12 -> x3, local copies, waits for them, and re-layouts: 158 us -> 6.01 us
    pallas_call x0 -> x1, Pallas kernels: none -> 109 us  [body(): pl.pallas_call(kernel, out_shape=(jax.ShapeDtypeStruct((MIDX, MIDX), F32)...]
    all_to_all x1 -> x0, blocking collectives: 93.3 us -> none  [body(): moved = lax.all_to_all(slab, 'mx', split_axis=2, concat_axis=0, tiled=True)]
    all_to_all x2 -> x0, other arithmetic: 88.6 us -> none  [the longest x1 80.4 us: body(): moved = lax.all_to_all(slab, 'mx', split_axis=2, concat_axis=0, tiled=True)]
    all_to_all x4 -> x0, local copies, waits for them, and re-layouts: 50.2 us -> none  [the longest x2 37.9 us: body(): moved = lax.all_to_all(slab, 'mx', split_axis=2, concat_axis=0, tiled=True)]
    dot_general x4 -> x0, matrix products: 36.2 us -> none  [the longest x1 15.8 us: body(): lax.dot_general(basis_x, flat, (((0,), (0,)), ((), ())), precision=high,...]
    all_to_all x1 -> x0, waiting for transfers between devices: 19.2 us -> none  [body(): lax.all_to_all(first, 'my', split_axis=2, concat_axis=1, tiled=True)]
    dot_general x2 -> x0, local copies, waits for them, and re-layouts: 17 us -> none  [body(): lax.dot_general(basis_x, flat, (((0,), (0,)), ((), ())), precision=high,...]
  transfers between devices with their start and end apart: 2 -> 1, of which waited for: 2 -> 1; matrix products, arithmetic and copies ran while one was open for 3% -> 0% of each run, Pallas kernels for 0% -> 0%
where the time goes in v1:
time: 273 us
  waiting for transfers between devices  144 us (53%)
  Pallas kernels  109 us (40%)
  between operations  14 us (5%)
  local copies, waits for them, and re-layouts  6.01 us (2%)
    psum x1, waiting for transfers between devices, body(): gx, gy = lax.psum((gx, gy), ('mx', 'my'))  144 us
    pallas_call x1, Pallas kernels, body(): pl.pallas_call(kernel, out_shape=(jax.ShapeDtypeStruct((MIDX, MIDX), F32)...  109 us
    unnamed x3, local copies, waits for them, and re-layouts  6.01 us
  transfers between devices with their start and end apart: 1, of which 1 were waited for; matrix products, arithmetic and copies ran while one was open for 0% of the time, Pallas kernels for 0%

profile of v1, /device:TPU:1, one launch (start us, length us, event | category | flops | bytes accessed | tf_op | source)
XLA Modules:
  0.0 272.7 jit_solution(14505183198086829575)
XLA Ops:
  7.2 0.0 all-reduce.3.cloned.1.call-start
  7.2 109.0 %shard_map.58 = (f32[192,192]{1,0:T(8,128)}, f32[192,192]{1,0:T(8,128)}, f32[50,60,60]{2,1,0:T(8,128)}) custom-call(f32[12,24,6400]{2,1,0:T(8,128)} %bitcast.4, f32[60,192]{1,0:T(8,128)} %bitcast.6, f32[60,192]{1,0:T(8,128)} %bitcast.7), custom_call_target="tpu_custom_call" | custom-call | tf_op jit(solution)/shard_map/pallas_call | solution.py:254
  116.3 0.0 all-reduce.3.cloned.1.call-update
  116.3 143.5 %all-reduce.3.cloned.1.call-done = (f32[192,192]{1,0:T(8,128)}, f32[192,192]{1,0:T(8,128)}) async-done(((f32[192,192]{1,0:T(8,128)}, f32[192,192]{1,0:T(8,128)}), (f32[192,192]{1,0:T(8,128)}, f32[192,192]{1,0:T(8,128)})) %all-reduce.3.cloned.1.call-update) | async-done | bytes 294928 | tf_op jit(solution)/shard_map/psum | solution.py:292
  259.8 1.6 copy.11
  261.4 1.6 copy.12
  263.0 2.8 %copy.13 = f32[60,60,50]{1,0,2:T(8,128)} copy(f32[60,60,50]{1,0,2:T(8,128)} %bitcast.5) | data formatting | bytes 1440000
Async XLA Ops:
  7.2 252.6 %all-reduce.3.cloned.1.call-start = ((), (), s32[]{:S(2)}) async-start(), calls=%async_computation | async-start | bytes 786432 | tf_op jit(solution)/shard_map/psum | solution.py:292
Sparse Core Ops, SparseCore 0:
  116.4 143.3 all-reduce.2

commit v2 on v1

--- a/solution.py
+++ b/solution.py
@@ -40,7 +40,9 @@
 def kernel(
     slab, bxt, byt, gx_out, gy_out, core_out,
     raw, s1a, s1b, r1a, r1b, g, ft, fs, fr, bb, bq, gxx, gxm, gyy, gym,
+    part, parts8, sums, parts16, full,
     raw_sem, own_sem, s1_send, s1_recv, s2_send, s2_recv, y_send, y_recv,
+    rs_send, rs_recv, bc_send, bc_recv, ag_send, ag_recv,
 ):
     mx, my = lax.axis_index("mx"), lax.axis_index("my")
     x, zh = lax.rem(mx, 4), mx // 4
@@ -63,6 +65,8 @@
     partners += [device(x, y, step(zz, d), core) for d in (1, 2, 3)]
     partners += [device(x, step(y, d), zz, c) for d in (1, 2, 3) for c in (0, 1)]
     partners += [device(x, y, zz, 1 - core)]
+    partners += [device(step(x, d), y, zz, 1 - core) for d in (1, 2, 3)]
+    partners += [device(x, step(y, d), step(zz, e), core) for d in (1, 2, 3) for e in (1, 2, 3)]
     for p in partners:
         pl.semaphore_signal(barrier, inc=1, device_id=p, device_id_type=MESH)
 
@@ -210,17 +214,75 @@
     project(CHUNKS - 1)
     hops3.append(spread(CHUNKS - 1))
 
-    for k in range(CHUNKS - 1):
-        for c in (0, 1):
-            remote(fs.at[k, c], fr.at[step(y, 3 - k), c], y_send.at[k, c], y_recv.at[k, c], device(x, y, zz, c)).wait_recv()
-    out, own = hops3[-1]
-    remote(fs.at[CHUNKS - 1, core], fr.at[y, 1 - core], y_send.at[CHUNKS - 1, 0], y_recv.at[CHUNKS - 1, 1 - core], device(x, y, zz, 1 - core)).wait_recv()
-    own[0].wait()
-
-    qhi, qlo = split(bq[...])
-    wide = 5
-
-    def finish(u, carry):
+    eights = [(d, e) for d in range(4) for e in range(2)]
+    sixteens = [(d, e) for d in range(4) for e in range(4)]
+    left = lax.broadcasted_iota(jnp.int32, (64, 128), 1) < 64
+
+    def own_rows(px, pc):
+        return pl.ds(pl.multiple_of((px * 2 + pc) * 24, 24), 24)
+
+    def scatter(i, main, cross, scale):
+        m = cross[...]
+        main[...] = (main[...] + (m + m.T)) * scale
+        part[i, 0:64] = main[0:64, 0:128]
+        high = jnp.concatenate([main[64:128, 128:192], jnp.zeros((64, 64), F32)], axis=1)
+        part[i, 64:128] = jnp.where(left, pltpu.roll(main[64:128, 0:128], 64, 1), pltpu.roll(high, 64, 1))
+        top = jnp.concatenate([main[0:64, 128:192], jnp.zeros((64, 64), F32)], axis=1)
+        end = jnp.concatenate([main[128:192, 128:192], jnp.zeros((64, 64), F32)], axis=1)
+        part[i, 128:192] = jnp.where(left, top, pltpu.roll(end, 64, 1))
+        out = []
+        for n, (d, e) in enumerate(eights):
+            if n:
+                px, pc = step(x, d), lax.rem(core + e, 2)
+                out.append(remote(part.at[i, own_rows(px, pc)], parts8.at[i, n - 1], rs_send.at[i, n - 1], rs_recv.at[i, n - 1], device(px, y, zz, pc)))
+                out[-1].start()
+        return out
+
+    def share(i, hop):
+        for c in hop:
+            c.wait_recv()
+        total = part[i, own_rows(x, core)]
+        for n in range(7):
+            total += parts8[i, n]
+        sums[i] = total
+        out = []
+        for n, (d, e) in enumerate(sixteens):
+            if n:
+                out.append(remote(sums.at[i], parts16.at[i, y * 4 + zz], bc_send.at[i, n - 1], bc_recv.at[i, n - 1], device(x, step(y, d), step(zz, e), core)))
+                out[-1].start()
+        parts16[i, y * 4 + zz] = total
+        return out
+
+    def gather(i, hop):
+        for c in hop:
+            c.wait_recv()
+        total = parts16[i, 0]
+        for n in range(1, 16):
+            total += parts16[i, n]
+        full[i, own_rows(x, core)] = total
+        out = []
+        for n, (d, e) in enumerate(eights):
+            if n:
+                px, pc = step(x, d), lax.rem(core + e, 2)
+                out.append(remote(full.at[i, own_rows(x, core)], full.at[i, own_rows(x, core)], ag_send.at[i, n - 1], ag_recv.at[i, n - 1], device(px, y, zz, pc)))
+                out[-1].start()
+        return out
+
+    def unfold(i, hop, ref):
+        for c in hop:
+            c.wait_recv()
+        p0, p1, p2 = full[i, 0:64], full[i, 64:128], full[i, 128:192]
+        t0 = full[i, 0:128].T
+        t2 = jnp.concatenate([p2, p2], axis=0).T
+        q1, q2 = pltpu.roll(p1, 64, 1), pltpu.roll(p2, 64, 1)
+        ref[0:64, 0:128] = p0
+        ref[0:64, 128:192] = p2[:, :64]
+        ref[64:128, 0:128] = jnp.where(left, t0[64:128], q1)
+        ref[64:128, 128:192] = q1[:, :64]
+        ref[128:192, 0:128] = jnp.where(left, t2[0:64], t0[64:128])
+        ref[128:192, 128:192] = q2[:, :64]
+
+    def columns(u):
         parts = []
         for e in range(wide):
             p = u * wide + e
@@ -229,9 +291,20 @@
                 a, b = fr[s, 0, p], fr[s, 1, p]
                 rows += [a[:JB], b[:JB], a[JB:], b[JB:]]
             parts.append(jnp.concatenate(rows, axis=0))
-        hi, lo = split(jnp.concatenate(parts, axis=1))
+        return split(jnp.concatenate(parts, axis=1))
+
+    wide = 5
+
+    def gram(u, carry):
+        hi, lo = columns(u)
         gyy[...] += dot(hi, hi, NT)
         gym[...] += dot(hi, lo, NT)
+        return carry
+
+    qhi, qlo = split(bq[...])
+
+    def finish(u, carry):
+        hi, lo = columns(u)
         c = dot(qhi, hi, NN) + (dot(qlo, hi, NN) + dot(qhi, lo, NN))
         for e in range(wide):
             p = u * wide + e
@@ -240,13 +313,28 @@
             core_out[p + HP] = pltpu.roll(v, 64, 1)[:RANK, :RANK]
         return carry
 
+    rs0 = scatter(0, gxx, gxm, 1.0 / (MIDY * COLS))
+    for k in range(CHUNKS - 1):
+        for c in (0, 1):
+            remote(fs.at[k, c], fr.at[step(y, 3 - k), c], y_send.at[k, c], y_recv.at[k, c], device(x, y, zz, c)).wait_recv()
+    out, own = hops3[-1]
+    remote(fs.at[CHUNKS - 1, core], fr.at[y, 1 - core], y_send.at[CHUNKS - 1, 0], y_recv.at[CHUNKS - 1, 1 - core], device(x, y, zz, 1 - core)).wait_recv()
+    own[0].wait()
+    lax.fori_loop(0, HP // wide, gram, 0)
+    rs1 = scatter(1, gyy, gym, 1.0 / (RANK * COLS))
+    bc0 = share(0, rs0)
     lax.fori_loop(0, HP // wide, finish, 0)
-    gx_out[...] = (gxx[...] + (gxm[...] + gxm[...].T)) * (1.0 / (MIDY * COLS))
-    gy_out[...] = (gyy[...] + (gym[...] + gym[...].T)) * (1.0 / (RANK * COLS))
+    bc1 = share(1, rs1)
+    ag0 = gather(0, bc0)
+    ag1 = gather(1, bc1)
+    unfold(0, ag0, gx_out)
+    unfold(1, ag1, gy_out)
 
     for out, _ in hops1 + hops2 + hops3:
         for c in out:
             c.wait_send()
+    for c in rs0 + rs1 + bc0 + bc1 + ag0 + ag1:
+        c.wait_send()
 
 
 def body(slab, basis_x, basis_y):
@@ -276,6 +364,11 @@
             pltpu.VMEM((MIDX, MIDX), F32),
             pltpu.VMEM((MIDY, MIDY), F32),
             pltpu.VMEM((MIDY, MIDY), F32),
+            pltpu.VMEM((2, 192, 128), F32),
+            pltpu.VMEM((2, 7, 24, 128), F32),
+            pltpu.VMEM((2, 24, 128), F32),
+            pltpu.VMEM((2, 16, 24, 128), F32),
+            pltpu.VMEM((2, 192, 128), F32),
             pltpu.SemaphoreType.DMA((JB,)),
             pltpu.SemaphoreType.DMA((CHUNKS, 4)),
             pltpu.SemaphoreType.DMA((CHUNKS, 2, 3)),
@@ -284,12 +377,17 @@
             pltpu.SemaphoreType.DMA((CHUNKS, 2, 3)),
             pltpu.SemaphoreType.DMA((CHUNKS, 2)),
             pltpu.SemaphoreType.DMA((CHUNKS, 2)),
+            pltpu.SemaphoreType.DMA((2, 7)),
+            pltpu.SemaphoreType.DMA((2, 7)),
+            pltpu.SemaphoreType.DMA((2, 15)),
+            pltpu.SemaphoreType.DMA((2, 15)),
+            pltpu.SemaphoreType.DMA((2, 7)),
+            pltpu.SemaphoreType.DMA((2, 7)),
         ],
         compiler_params=pltpu.CompilerParams(
             collective_id=0, has_side_effects=True, vmem_limit_bytes=58 * 2**20
         ),
     )(jnp.transpose(slab, (1, 0, 2)), basis_x.T, basis_y.T)
-    gx, gy = lax.psum((gx, gy), ("mx", "my"))
     return gx, gy, jnp.transpose(core, (1, 2, 0))
 
 

time: 273 us -> 132 us (0.48)
  waiting for transfers between devices: 144 us -> 0 us
  Pallas kernels: 109 us -> 125 us
  between operations: 14 us -> 0.64 us
    psum x1 -> x0, waiting for transfers between devices: 144 us -> none  [body(): gx, gy = lax.psum((gx, gy), ('mx', 'my'))]
    pallas_call x1, Pallas kernels: 109 us -> 125 us  [body(): pl.pallas_call(kernel, out_shape=(jax.ShapeDtypeStruct((MIDX, MIDX), F32)...]
  transfers between devices with their start and end apart: 1 -> 0, of which waited for: 1 -> 0; matrix products, arithmetic and copies ran while one was open for 0% -> 0% of each run, Pallas kernels for 0% -> 0%
where the time goes in v2:
time: 132 us; the launch traced here: 131 us
  Pallas kernels  125 us (95%)
  local copies, waits for them, and re-layouts  6.01 us (5%)
    pallas_call x1, Pallas kernels, body(): pl.pallas_call(kernel, out_shape=(jax.ShapeDtypeStruct((MIDX, MIDX), F32)...  125 us
    unnamed x3, local copies, waits for them, and re-layouts  6.01 us

profile of v2, /device:TPU:1, one launch (start us, length us, event | category | flops | bytes accessed | tf_op | source)
XLA Modules:
  0.0 131.4 jit_solution(7614765439933680107)
XLA Ops:
  0.6 124.8 %shard_map.58 = (f32[192,192]{1,0:T(8,128)}, f32[192,192]{1,0:T(8,128)}, f32[50,60,60]{2,1,0:T(8,128)}) custom-call(f32[12,24,6400]{2,1,0:T(8,128)} %bitcast.4, f32[60,192]{1,0:T(8,128)} %bitcast.6, f32[60,192]{1,0:T(8,128)} %bitcast.7), custom_call_target="tpu_custom_call" | custom-call | tf_op jit(solution)/shard_map/pallas_call | solution.py:342
  125.4 1.6 %copy.9 = f32[192,192]{1,0:T(8,128)} copy(f32[192,192]{1,0:T(8,128)} %get-tuple-element.12) | data formatting | bytes 294912
  127.1 1.6 %copy.10 = f32[192,192]{1,0:T(8,128)} copy(f32[192,192]{1,0:T(8,128)} %get-tuple-element.13) | data formatting | bytes 294912
  128.7 2.8 %copy.11 = f32[60,60,50]{1,0,2:T(8,128)} copy(f32[60,60,50]{1,0,2:T(8,128)} %bitcast.5) | data formatting | bytes 1440000

commit v3 on v0

v3 whole, which is shorter than its diff:
```python
import jax
import jax.numpy as jnp
from jax import lax
from jax.experimental import pallas as pl
from jax.experimental.pallas import tpu as pltpu
from jax.sharding import PartitionSpec as P

MESH = pl.DeviceIdType.MESH
F32 = jnp.float32
BF16 = jnp.bfloat16

MIDX = 192
MIDY = 192
RANK = 60
COLS = 6400
JB = 12
IB = 24
OWN = 50
PAIR = 2 * OWN
HP = OWN // 2
CHUNKS = 4
SEGS = CHUNKS * JB
PARTS = (((0, 5), (5, 5)), ((10, 5), (15, 5)), ((20, 5), (25, 4)), ((29, 3), (32, 3)), ((35, 1), (36, 2)))
TILES = 38
LANES = TILES // 2 * 128
STARTS = ((0, 0), (5, 5), (10, 10), (15, 14), (18, 17))
READY = {0: 0, 1: 1, 2: 2, 4: 3}

NT = (((1,), (1,)), ((), ()))
NN = (((1,), (0,)), ((), ()))


def split(a):
    hi = a.astype(BF16)
    return hi, (a - hi.astype(F32)).astype(BF16)


def dot(a, b, dims):
    return lax.dot_general(a, b, dims, preferred_element_type=F32)


def kernel(
    slab, bxt, byt, full_out, core_out,
    raw, s1a, s1b, r1a, r1b, g, ft, fs, fr, bases_v, bb, bq, gxx, gxm, gyy, gym,
    part, parts8, sums, parts16, full, core_v,
    load_sem, hop_send, s1_recv, s2_recv, y_send, y_recv, store_sem,
    rs_send, rs_recv, bc_send, bc_recv, ag_send, ag_recv,
):
    mx, my = lax.axis_index("mx"), lax.axis_index("my")
    x, zh = lax.rem(mx, 4), mx // 4
    y, zl, core = my // 4, lax.rem(my // 2, 2), lax.rem(my, 2)
    zz = zl * 2 + zh

    def device(px, py, pz, pc):
        return (lax.rem(pz, 2) * 4 + px, py * 4 + (pz // 2) * 2 + pc)

    def step(v, d):
        return lax.rem(v + d, 4)

    barrier = pltpu.get_barrier_semaphore()
    partners = [device(step(x, d), y, zz, core) for d in (1, 2, 3)]
    partners += [device(x, y, step(zz, d), core) for d in (1, 2, 3)]
    partners += [device(x, step(y, d), zz, c) for d in (1, 2, 3) for c in (0, 1)]
    partners += [device(x, y, zz, 1 - core)]
    for p in partners:
        pl.semaphore_signal(barrier, inc=1, device_id=p, device_id_type=MESH)


    early, late = pl.ds(0, 7), pl.ds(7, JB - 7)
    loads = [pltpu.make_async_copy(slab.at[r], raw.at[r], load_sem.at[n]) for n, r in enumerate((early, late))]
    bases = [pltpu.make_async_copy(b, bases_v.at[n], load_sem.at[2]) for n, b in enumerate((bxt, byt))]
    for c in loads + bases:
        c.start()

    def landed(ref, sem):
        pltpu.make_async_copy(ref, ref, sem).wait()

    lane = lax.broadcasted_iota(jnp.int32, (IB, 128), 1)

    def lanes(t, h):
        return pl.ds(STARTS[t][h] * 128, PARTS[t][h][1] * 128)

    def pack(t, h, px, pz, dst):
        first, count = PARTS[t][h]
        tiles = [None] * count
        where = {}
        for n in range(first * 128 // PAIR, min(SEGS, -(-(first + count) * 128 // PAIR))):
            k, j = divmod(n, JB)
            if k not in where:
                off = PAIR * ((lax.rem(pz, 2) * 4 + px) * 8 + step(y, 1 + k) * 2 + pz // 2)
                t0 = off // 128
                t1 = jnp.minimum(t0 + 1, COLS // 128 - 1)
                where[k] = (pl.multiple_of(t0 * 128, 128), pl.multiple_of(t1 * 128, 128), off - t0 * 128)
            l0, l1, s = where[k]
            d, w = (n * PAIR) % 128, (n * PAIR) // 128 - first
            sh = lax.rem(d - s + 128, 128)
            v0 = pltpu.roll(raw[j, :, pl.ds(l0, 128)], sh, 1)
            v1 = pltpu.roll(raw[j, :, pl.ds(l1, 128)], sh, 1)
            v = jnp.where(lax.rem(lane - d + 128, 128) < 128 - s, v0, v1)
            if 0 <= w < count:
                tiles[w] = v if tiles[w] is None else jnp.where(lane < d, tiles[w], v)
            if d + PAIR > 128 and w + 1 < count:
                tiles[w + 1] = v
        if first + count == TILES:
            tiles[-1] = jnp.where(lane < SEGS * PAIR - (TILES - 1) * 128, tiles[-1], 0.0)
        for w in range(count):
            lo = (STARTS[t][h] + w) * 128
            dst[:, lo : lo + 128] = tiles[w]

    def pack_a(t, px, dst):
        lax.fori_loop(0, 4, lambda pz, c: (pack(t, 0, px, pz, dst.at[pz]), c)[1], 0)

    def pack_b(t, pz, dst):
        lax.fori_loop(0, 4, lambda px, c: (pack(t, 1, px, pz, dst.at[px]), c)[1], 0)

    def remote(src, dst, ssem, rsem, dev):
        return pltpu.make_async_remote_copy(
            src_ref=src, dst_ref=dst, send_sem=ssem, recv_sem=rsem, device_id=dev, device_id_type=MESH
        )

    def first_copy(t, h, d):
        w = lanes(t, h)
        if h == 0:
            px = step(x, d)
            return remote(s1a.at[px, :, :, w], r1a.at[x, :, :, w], hop_send.at[0], s1_recv.at[t, 0], device(px, y, zz, core))
        pz = step(zz, d)
        return remote(s1b.at[pz, :, :, w], r1b.at[zz, :, :, w], hop_send.at[1], s1_recv.at[t, 1], device(x, y, pz, core))

    def send_a(t, d):
        px = step(x, d)
        pack_a(t, px, s1a.at[px])
        first_copy(t, 0, d).start()

    def send_b(t, d):
        pz = step(zz, d)
        pack_b(t, pz, s1b.at[pz])
        first_copy(t, 1, d).start()

    def first_hop(t, begun=False):
        def message(n, carry):
            d = 2 - n + 3 * (n // 2)
            send_a(t, d)
            send_b(t, d)
            return carry

        lax.fori_loop(1 if begun else 0, 3, message, 0)
        pack_a(t, x, r1a.at[x])
        pack_b(t, zz, r1b.at[zz])

    def second_hop(t):
        wa, wb = lanes(t, 0), lanes(t, 1)
        landed(r1a.at[0:3, :, :, wa], s1_recv.at[t, 0])
        landed(r1b.at[0:3, :, :, wb], s1_recv.at[t, 1])
        for d in (2, 1, 3):
            px, pz = step(x, d), step(zz, d)
            remote(r1a.at[:, pz, :, wa], g.at[0, zz, :, :, wa], hop_send.at[2], s2_recv.at[t, 0], device(x, y, pz, core)).start()
            remote(r1b.at[:, px, :, wb], g.at[1, :, x, :, wb], hop_send.at[3], s2_recv.at[t, 1], device(px, y, zz, core)).start()
        pltpu.make_async_copy(r1a.at[:, zz, :, wa], g.at[0, zz, :, :, wa], s2_recv.at[t, 0]).start()
        pltpu.make_async_copy(r1b.at[:, x, :, wb], g.at[1, :, x, :, wb], s2_recv.at[t, 1]).start()

    low = lax.broadcasted_iota(jnp.int32, (JB, 128), 1) < 64

    def project(t):
        for h in (0, 1):
            first, count = PARTS[t][h]

            def block(v, carry, h=h, first=first, count=count):
                a = g[h, pl.ds(v * 2, 2), :, :, lanes(t, h)].reshape(MIDX, count * 128)
                hi, lo = split(a)
                gxx[...] += dot(hi, hi, NT)
                gxm[...] += dot(hi, lo, NT)
                bhi, blo = split(bb[...])
                f = dot(bhi, hi, NN) + (dot(blo, hi, NN) + dot(bhi, lo, NN))
                ft[v, first * 128 : (first + count) * 128, :] = f.T
                return carry

            lax.fori_loop(0, 2, block, 0)

    def pair(k):
        def pairs(p, carry):
            for c in (0, 1):
                for v in (0, 1):
                    row = k * JB * PAIR + c * OWN + p
                    a = ft[v, pl.ds(row, JB, PAIR), :]
                    b = ft[v, pl.ds(row + HP, JB, PAIR), :]
                    fs[k, c, p, v * JB : (v + 1) * JB, :] = jnp.where(low, a, b)
            return carry

        lax.fori_loop(0, HP, pairs, 0)

    def spread(k):
        py = step(y, 1 + k)
        if k < CHUNKS - 1:
            for c in (0, 1):
                remote(fs.at[k, c], fr.at[y, core], y_send.at[0], y_recv.at[k], device(x, py, zz, c)).start()
        else:
            c = 1 - core
            remote(fs.at[k, c], fr.at[y, core], y_send.at[1], y_recv.at[k], device(x, y, zz, c)).start()
            pltpu.make_async_copy(fs.at[k, core], fr.at[y, core], y_recv.at[k]).start()

    def chunk(t):
        landed(g.at[0, :, :, :, lanes(t, 0)], s2_recv.at[t, 0])
        landed(g.at[1, :, :, :, lanes(t, 1)], s2_recv.at[t, 1])
        project(t)
        if t in READY:
            pair(READY[t])
            spread(READY[t])

    loads[0].wait()
    pl.semaphore_wait(barrier, len(partners))
    send_a(0, 2)
    loads[1].wait()
    send_b(0, 2)
    first_hop(0, True)
    first_hop(1)
    landed(bases_v, load_sem.at[2])
    bb[...] = jnp.zeros_like(bb)
    bb[0:RANK, :] = bases_v[0]
    bb[64 : 64 + RANK, :] = bases_v[0]
    bq[...] = jnp.zeros_like(bq)
    bq[0:RANK, :] = bases_v[1]
    for acc in (gxx, gxm, gyy, gym):
        acc[...] = jnp.zeros_like(acc)
    second_hop(0)
    first_hop(2)
    second_hop(1)
    chunk(0)
    second_hop(2)
    first_hop(3)
    first_hop(4)
    chunk(1)
    chunk(2)
    second_hop(3)
    second_hop(4)
    chunk(3)
    chunk(4)

    eights = [(d, e) for d in range(4) for e in range(2)]
    sixteens = [(d, e) for d in (2, 1, 3, 0) for e in (2, 1, 3, 0)]
    left = lax.broadcasted_iota(jnp.int32, (64, 128), 1) < 64

    def own_rows(px, pc):
        return pl.ds(pl.multiple_of((px * 2 + pc) * 24, 24), 24)

    def scatter(i, main, cross, scale):
        m = cross[...]
        main[...] = (main[...] + (m + m.T)) * scale
        part[i, 0:64] = main[0:64, 0:128]
        high = jnp.concatenate([main[64:128, 128:192], jnp.zeros((64, 64), F32)], axis=1)
        part[i, 64:128] = jnp.where(left, pltpu.roll(main[64:128, 0:128], 64, 1), pltpu.roll(high, 64, 1))
        top = jnp.concatenate([main[0:64, 128:192], jnp.zeros((64, 64), F32)], axis=1)
        end = jnp.concatenate([main[128:192, 128:192], jnp.zeros((64, 64), F32)], axis=1)
        part[i, 128:192] = jnp.where(left, top, pltpu.roll(end, 64, 1))
        for d, e in eights[::-1]:
            if d or e:
                px, pc = step(x, d), lax.rem(core + e, 2)
                remote(part.at[i, own_rows(px, pc)], parts8.at[i, d * 2 + e - 1], rs_send.at[i], rs_recv.at[i], device(px, y, zz, pc)).start()

    def share(i):
        landed(parts8.at[i], rs_recv.at[i])
        total = part[i, own_rows(x, core)]
        for n in range(7):
            total += parts8[i, n]
        sums[i] = total
        for d, e in sixteens:
            if d or e:
                remote(sums.at[i], parts16.at[i, y * 4 + zz], bc_send.at[i], bc_recv.at[i], device(x, step(y, d), step(zz, e), core)).start()
        parts16[i, y * 4 + zz] = total

    def gather(i):
        landed(parts16.at[i, 0:15], bc_recv.at[i])
        total = parts16[i, 0]
        for n in range(1, 16):
            total += parts16[i, n]
        full[i, own_rows(x, core)] = total
        for d, e in eights[::-1]:
            if d or e:
                px, pc = step(x, d), lax.rem(core + e, 2)
                remote(full.at[i, own_rows(x, core)], full.at[i, own_rows(x, core)], ag_send.at[i], ag_recv.at[i], device(px, y, zz, pc)).start()

    wide = 5

    def columns(u):
        parts = []
        for e in range(wide):
            p = u * wide + e
            rows = []
            for s in range(4):
                a, b = fr[s, 0, p], fr[s, 1, p]
                rows += [a[:JB], b[:JB], a[JB:], b[JB:]]
            parts.append(jnp.concatenate(rows, axis=0))
        return split(jnp.concatenate(parts, axis=1))

    def gram(u, carry):
        hi, lo = columns(u)
        gyy[...] += dot(hi, hi, NT)
        gym[...] += dot(hi, lo, NT)
        return carry

    qhi, qlo = split(bq[...])

    def finish(u, carry):
        hi, lo = columns(u)
        c = dot(qhi, hi, NN) + (dot(qlo, hi, NN) + dot(qhi, lo, NN))
        for e in range(wide):
            p = u * wide + e
            core_v[p] = c[:, e * 128 : (e + 1) * 128]
        return carry

    for k in range(CHUNKS):
        landed(fr.at[0], y_recv.at[k])
    scatter(0, gxx, gxm, 1.0 / (MIDY * COLS))
    lax.fori_loop(0, HP // wide, gram, 0)
    scatter(1, gyy, gym, 1.0 / (RANK * COLS))
    share(0)
    lax.fori_loop(0, HP // wide, finish, 0)
    core_store = pltpu.make_async_copy(core_v, core_out, store_sem.at[0])
    core_store.start()
    share(1)
    gather(0)
    gather(1)
    landed(s1a.at[0:3], hop_send.at[0])
    landed(s1b.at[0:3], hop_send.at[1])
    landed(r1a.at[0:3], hop_send.at[2])
    landed(r1b.at[0:3], hop_send.at[3])
    landed(fs.at[0:3], y_send.at[0])
    landed(fs.at[3, 0], y_send.at[1])
    for i in (0, 1):
        landed(parts8.at[i], rs_send.at[i])
        landed(parts16.at[i, 0:15], bc_send.at[i])
    core_store.wait()
    for i in (0, 1):
        landed(full.at[i, 0:168], ag_recv.at[i])
    store = pltpu.make_async_copy(full, full_out, store_sem.at[1])
    store.start()
    for i in (0, 1):
        landed(full.at[i, 0:168], ag_send.at[i])
    store.wait()


def unfold(full, core, gx_out, gy_out, core_out):
    left = lax.broadcasted_iota(jnp.int32, (64, 128), 1) < 64
    for i, ref in enumerate((gx_out, gy_out)):
        p0, p1, p2 = full[i, 0:64], full[i, 64:128], full[i, 128:192]
        t0 = full[i, 0:128].T
        t2 = jnp.concatenate([p2, p2], axis=0).T
        q1, q2 = pltpu.roll(p1, 64, 1), pltpu.roll(p2, 64, 1)
        ref[0:64, 0:128] = p0
        ref[0:64, 128:192] = p2[:, :64]
        ref[64:128, 0:128] = jnp.where(left, t0[64:128], q1)
        ref[64:128, 128:192] = q1[:, :64]
        ref[128:192, 0:128] = jnp.where(left, t2[0:64], t0[64:128])
        ref[128:192, 128:192] = q2[:, :64]
    for p in range(HP):
        v = core[p]
        core_out[p] = v[:RANK, :RANK]
        core_out[p + HP] = pltpu.roll(v, 64, 1)[:RANK, :RANK]


def body(slab, basis_x, basis_y):
    anywhere = pl.BlockSpec(memory_space=pl.ANY)
    vmem = pl.BlockSpec(memory_space=pltpu.VMEM)
    full, core = pl.pallas_call(
        kernel,
        out_shape=(
            jax.ShapeDtypeStruct((2, 192, 128), F32),
            jax.ShapeDtypeStruct((HP, 64, 128), F32),
        ),
        in_specs=[anywhere] * 3,
        out_specs=(anywhere, anywhere),
        scratch_shapes=[
            pltpu.VMEM((JB, IB, COLS), F32),
            pltpu.VMEM((4, 4, IB, LANES), F32),
            pltpu.VMEM((4, 4, IB, LANES), F32),
            pltpu.VMEM((4, 4, IB, LANES), F32),
            pltpu.VMEM((4, 4, IB, LANES), F32),
            pltpu.VMEM((2, 4, 4, IB, LANES), F32),
            pltpu.VMEM((2, TILES * 128, 128), F32),
            pltpu.VMEM((CHUNKS, 2, HP, 2 * JB, 128), F32),
            pltpu.VMEM((4, 2, HP, 2 * JB, 128), F32),
            pltpu.VMEM((2, RANK, MIDX), F32),
            pltpu.VMEM((128, MIDX), F32),
            pltpu.VMEM((64, MIDY), F32),
            pltpu.VMEM((MIDX, MIDX), F32),
            pltpu.VMEM((MIDX, MIDX), F32),
            pltpu.VMEM((MIDY, MIDY), F32),
            pltpu.VMEM((MIDY, MIDY), F32),
            pltpu.VMEM((2, 192, 128), F32),
            pltpu.VMEM((2, 7, 24, 128), F32),
            pltpu.VMEM((2, 24, 128), F32),
            pltpu.VMEM((2, 16, 24, 128), F32),
            pltpu.VMEM((2, 192, 128), F32),
            pltpu.VMEM((HP, 64, 128), F32),
            pltpu.SemaphoreType.DMA((3,)),
            pltpu.SemaphoreType.DMA((4,)),
            pltpu.SemaphoreType.DMA((len(PARTS), 2)),
            pltpu.SemaphoreType.DMA((len(PARTS), 2)),
            pltpu.SemaphoreType.DMA((2,)),
            pltpu.SemaphoreType.DMA((CHUNKS,)),
            pltpu.SemaphoreType.DMA((2,)),
            pltpu.SemaphoreType.DMA((2,)),
            pltpu.SemaphoreType.DMA((2,)),
            pltpu.SemaphoreType.DMA((2,)),
            pltpu.SemaphoreType.DMA((2,)),
            pltpu.SemaphoreType.DMA((2,)),
            pltpu.SemaphoreType.DMA((2,)),
        ],
        compiler_params=pltpu.CompilerParams(
            collective_id=0, has_side_effects=True, vmem_limit_bytes=58 * 2**20
        ),
    )(jnp.transpose(slab, (1, 0, 2)), basis_x.T, basis_y.T)
    gx, gy, core = pl.pallas_call(
        unfold,
        out_shape=(
            jax.ShapeDtypeStruct((MIDX, MIDX), F32),
            jax.ShapeDtypeStruct((MIDY, MIDY), F32),
            jax.ShapeDtypeStruct((OWN, RANK, RANK), F32),
        ),
        in_specs=[vmem, vmem],
        out_specs=(vmem, vmem, vmem),
    )(full, core)
    return gx, gy, jnp.transpose(core, (1, 2, 0))


def solution(mesh):
    return jax.shard_map(
        body,
        mesh=mesh,
        in_specs=(P("mx", "my", None), P(), P()),
        out_specs=(P(), P(), P(None, None, ("mx", "my"))),
        check_vma=False,
    )
```

time: 640 us -> 116 us (0.18); the launches traced: 630 us -> 116 us
  local copies, waits for them, and re-layouts: 235 us -> 0 us
  waiting for transfers between devices: 155 us -> 0 us
  Pallas kernels: 0 us -> 115 us
  blocking collectives: 93.3 us -> 0 us
  other arithmetic: 88.6 us -> 0 us
  matrix products: 36.2 us -> 0 us
  between operations: 14.5 us -> 0.64 us
  starting transfers between devices: 7.23 us -> 0 us
    unnamed x12 -> x0, local copies, waits for them, and re-layouts: 158 us -> none
    psum x1 -> x0, waiting for transfers between devices: 136 us -> none  [body(): gram_x = lax.psum(part_x, ('mx', 'my'))]
    pallas_call x0 -> x2, Pallas kernels: none -> 115 us  [the longest x1 112 us: body(): pl.pallas_call(kernel, out_shape=(jax.ShapeDtypeStruct((2, 192, 128), F32...]
    all_to_all x1 -> x0, blocking collectives: 93.3 us -> none  [body(): moved = lax.all_to_all(slab, 'mx', split_axis=2, concat_axis=0, tiled=True)]
    all_to_all x2 -> x0, other arithmetic: 88.6 us -> none  [the longest x1 80.4 us: body(): moved = lax.all_to_all(slab, 'mx', split_axis=2, concat_axis=0, tiled=True)]
    all_to_all x4 -> x0, local copies, waits for them, and re-layouts: 50.2 us -> none  [the longest x2 37.9 us: body(): moved = lax.all_to_all(slab, 'mx', split_axis=2, concat_axis=0, tiled=True)]
    dot_general x4 -> x0, matrix products: 36.2 us -> none  [the longest x1 15.8 us: body(): lax.dot_general(basis_x, flat, (((0,), (0,)), ((), ())), precision=high,...]
    all_to_all x1 -> x0, waiting for transfers between devices: 19.2 us -> none  [body(): lax.all_to_all(first, 'my', split_axis=2, concat_axis=1, tiled=True)]
  transfers between devices with their start and end apart: 2 -> 0, of which waited for: 2 -> 0; matrix products, arithmetic and copies ran while one was open for 3% -> 0% of each run, Pallas kernels for 0% -> 0%
where the time goes in v3:
time: 116 us
  Pallas kernels  115 us (99%)
    pallas_call x1, Pallas kernels, body(): pl.pallas_call(kernel, out_shape=(jax.ShapeDtypeStruct((2, 192, 128), F32...  112 us
    pallas_call x1, Pallas kernels, body(): pl.pallas_call(unfold, out_shape=(jax.ShapeDtypeStruct((MIDX, MIDX), F32)...  2.82 us

profile of v3, /device:TPU:1, one launch (start us, length us, event | category | flops | bytes accessed | tf_op | source)
XLA Modules:
  0.0 115.7 jit_solution(12535082572759243122)
XLA Ops:
  0.6 112.3 %shard_map.58 = (f32[2,192,128]{2,1,0:T(8,128)}, f32[25,64,128]{2,1,0:T(8,128)}) custom-call(f32[12,24,6400]{2,1,0:T(8,128)} %bitcast.4, f32[60,192]{1,0:T(8,128)} %bitcast.5, f32[60,192]{1,0:T(8,128)} %bitcast.6), custom_call_target="tpu_custom_call" | custom-call | tf_op jit(solution)/shard_map/pallas_call | solution.py:363
  112.9 2.8 %shard_map.59 = (f32[192,192]{1,0:T(8,128)}, f32[192,192]{1,0:T(8,128)}, f32[50,60,60]{2,1,0:T(8,128)}) custom-call(f32[2,192,128]{2,1,0:T(8,128)} %get-tuple-element.8.full, f32[25,64,128]{2,1,0:T(8,128)} %get-tuple-element.9.core), custom_call_target="tpu_custom_call" | custom-call | tf_op jit(solution)/shard_map/pallas_call | solution.py:412

commit v4 on v3

--- a/solution.py
+++ b/solution.py
@@ -19,12 +19,21 @@
 PAIR = 2 * OWN
 HP = OWN // 2
 CHUNKS = 4
-SEGS = CHUNKS * JB
-PARTS = (((0, 5), (5, 5)), ((10, 5), (15, 5)), ((20, 5), (25, 4)), ((29, 3), (32, 3)), ((35, 1), (36, 2)))
+EARLY, LATE = 34, 16
+EP, LP = EARLY // 2, LATE // 2
+RUNS = [(k * JB * PAIR + j * PAIR, k, j, 0, PAIR) for k in range(CHUNKS - 1) for j in range(JB)]
+FIRST = (CHUNKS - 1) * JB * PAIR
+RUNS += [(FIRST + (2 * j + i) * EARLY, CHUNKS - 1, j, i * (PAIR - EARLY), EARLY) for j in range(JB) for i in (0, 1)]
+FILLED = FIRST + 2 * JB * EARLY
+SECOND = -(-FILLED // 128) * 128
+RUNS += [(SECOND + j * 2 * LATE, CHUNKS - 1, j, EARLY, 2 * LATE) for j in range(JB)]
+PARTS = (
+    ((0, 2), (2, 2)), ((4, 3), (7, 3)), ((10, 5), (15, 5)),
+    ((20, 5), (25, 4)), ((29, 3), (32, 3)), ((35, 1), (36, 2)),
+)
 TILES = 38
 LANES = TILES // 2 * 128
-STARTS = ((0, 0), (5, 5), (10, 10), (15, 14), (18, 17))
-READY = {0: 0, 1: 1, 2: 2, 4: 3}
+STARTS = ((0, 0), (2, 2), (5, 5), (10, 10), (15, 14), (18, 17))
 
 NT = (((1,), (1,)), ((), ()))
 NN = (((1,), (0,)), ((), ()))
@@ -61,14 +70,14 @@
     partners = [device(step(x, d), y, zz, core) for d in (1, 2, 3)]
     partners += [device(x, y, step(zz, d), core) for d in (1, 2, 3)]
     partners += [device(x, step(y, d), zz, c) for d in (1, 2, 3) for c in (0, 1)]
-    partners += [device(x, y, zz, 1 - core)]
+    partners += [device(step(x, d), y, zz, 1 - core) for d in range(4)]
     for p in partners:
         pl.semaphore_signal(barrier, inc=1, device_id=p, device_id_type=MESH)
 
 
-    early, late = pl.ds(0, 7), pl.ds(7, JB - 7)
-    loads = [pltpu.make_async_copy(slab.at[r], raw.at[r], load_sem.at[n]) for n, r in enumerate((early, late))]
-    bases = [pltpu.make_async_copy(b, bases_v.at[n], load_sem.at[2]) for n, b in enumerate((bxt, byt))]
+    rows = (pl.ds(0, 3), pl.ds(3, 3), pl.ds(6, 6))
+    loads = [pltpu.make_async_copy(slab.at[r], raw.at[r], load_sem.at[n]) for n, r in enumerate(rows)]
+    bases = [pltpu.make_async_copy(b, bases_v.at[n], load_sem.at[3]) for n, b in enumerate((bxt, byt))]
     for c in loads + bases:
         c.start()
 
@@ -83,26 +92,28 @@
     def pack(t, h, px, pz, dst):
         first, count = PARTS[t][h]
         tiles = [None] * count
-        where = {}
-        for n in range(first * 128 // PAIR, min(SEGS, -(-(first + count) * 128 // PAIR))):
-            k, j = divmod(n, JB)
-            if k not in where:
-                off = PAIR * ((lax.rem(pz, 2) * 4 + px) * 8 + step(y, 1 + k) * 2 + pz // 2)
-                t0 = off // 128
-                t1 = jnp.minimum(t0 + 1, COLS // 128 - 1)
-                where[k] = (pl.multiple_of(t0 * 128, 128), pl.multiple_of(t1 * 128, 128), off - t0 * 128)
-            l0, l1, s = where[k]
-            d, w = (n * PAIR) % 128, (n * PAIR) // 128 - first
+        base = {}
+        for at, k, j, col, size in RUNS:
+            d, w = at % 128, at // 128 - first
+            if w >= count or at + size <= first * 128:
+                continue
+            if k not in base:
+                base[k] = PAIR * ((lax.rem(pz, 2) * 4 + px) * 8 + step(y, 1 + k) * 2 + pz // 2)
+            off = base[k] + col
+            t0 = off // 128
+            t1 = jnp.minimum(t0 + 1, COLS // 128 - 1)
+            s = off - t0 * 128
             sh = lax.rem(d - s + 128, 128)
-            v0 = pltpu.roll(raw[j, :, pl.ds(l0, 128)], sh, 1)
-            v1 = pltpu.roll(raw[j, :, pl.ds(l1, 128)], sh, 1)
+            v0 = pltpu.roll(raw[j, :, pl.ds(pl.multiple_of(t0 * 128, 128), 128)], sh, 1)
+            v1 = pltpu.roll(raw[j, :, pl.ds(pl.multiple_of(t1 * 128, 128), 128)], sh, 1)
             v = jnp.where(lax.rem(lane - d + 128, 128) < 128 - s, v0, v1)
-            if 0 <= w < count:
+            if w >= 0:
                 tiles[w] = v if tiles[w] is None else jnp.where(lane < d, tiles[w], v)
-            if d + PAIR > 128 and w + 1 < count:
+            if d + size > 128 and w + 1 < count:
                 tiles[w + 1] = v
-        if first + count == TILES:
-            tiles[-1] = jnp.where(lane < SEGS * PAIR - (TILES - 1) * 128, tiles[-1], 0.0)
+        if first <= FILLED // 128 < first + count:
+            w = FILLED // 128 - first
+            tiles[w] = jnp.where(lane < FILLED % 128, tiles[w], 0.0)
         for w in range(count):
             lo = (STARTS[t][h] + w) * 128
             dst[:, lo : lo + 128] = tiles[w]
@@ -161,59 +172,65 @@
     low = lax.broadcasted_iota(jnp.int32, (JB, 128), 1) < 64
 
     def project(t):
-        for h in (0, 1):
-            first, count = PARTS[t][h]
-
-            def block(v, carry, h=h, first=first, count=count):
-                a = g[h, pl.ds(v * 2, 2), :, :, lanes(t, h)].reshape(MIDX, count * 128)
-                hi, lo = split(a)
-                gxx[...] += dot(hi, hi, NT)
-                gxm[...] += dot(hi, lo, NT)
-                bhi, blo = split(bb[...])
-                f = dot(bhi, hi, NN) + (dot(blo, hi, NN) + dot(bhi, lo, NN))
-                ft[v, first * 128 : (first + count) * 128, :] = f.T
-                return carry
-
-            lax.fori_loop(0, 2, block, 0)
-
-    def pair(k):
+        both = [(h, v) for h in (0, 1) for v in (0, 1)]
+        for group in (both,) if t > 3 else (both[:2], both[2:]):
+            blocks = [g[h, v * 2 : v * 2 + 2, :, :, lanes(t, h)].reshape(MIDX, -1) for h, v in group]
+            hi, lo = split(jnp.concatenate(blocks, axis=1))
+            gxx[...] += dot(hi, hi, NT)
+            gxm[...] += dot(hi, lo, NT)
+            bhi, blo = split(bb[...])
+            f = dot(bhi, hi, NN) + (dot(blo, hi, NN) + dot(bhi, lo, NN))
+            at = 0
+            for h, v in group:
+                first, size = PARTS[t][h][0] * 128, PARTS[t][h][1] * 128
+                ft[v, first : first + size, :] = f[:, at : at + size].T
+                at += size
+
+    def pair(k, c, row, gap, stride, at, n):
         def pairs(p, carry):
-            for c in (0, 1):
-                for v in (0, 1):
-                    row = k * JB * PAIR + c * OWN + p
-                    a = ft[v, pl.ds(row, JB, PAIR), :]
-                    b = ft[v, pl.ds(row + HP, JB, PAIR), :]
-                    fs[k, c, p, v * JB : (v + 1) * JB, :] = jnp.where(low, a, b)
+            for v in (0, 1):
+                a = ft[v, pl.ds(row + p, JB, stride), :]
+                b = ft[v, pl.ds(row + gap + p, JB, stride), :]
+                fs[k, c, at + p, v * JB : (v + 1) * JB, :] = jnp.where(low, a, b)
             return carry
 
-        lax.fori_loop(0, HP, pairs, 0)
+        lax.fori_loop(0, n, pairs, 0)
 
     def spread(k):
         py = step(y, 1 + k)
-        if k < CHUNKS - 1:
-            for c in (0, 1):
-                remote(fs.at[k, c], fr.at[y, core], y_send.at[0], y_recv.at[k], device(x, py, zz, c)).start()
-        else:
-            c = 1 - core
-            remote(fs.at[k, c], fr.at[y, core], y_send.at[1], y_recv.at[k], device(x, y, zz, c)).start()
-            pltpu.make_async_copy(fs.at[k, core], fr.at[y, core], y_recv.at[k]).start()
+        for c in (0, 1):
+            row = k * JB * PAIR + c * (OWN + LATE)
+            pair(k, c, row, EP, PAIR, 0, EP)
+            pair(k, c, k * JB * PAIR + (OWN if c else EARLY), LP, PAIR, EP, LP)
+            remote(fs.at[k, c], fr.at[y, core], y_send.at[0], y_recv.at[k], device(x, py, zz, c)).start()
+
+    def swap(part):
+        k, c = CHUNKS - 1, 1 - core
+        at, n = ((0, EP), (EP, LP))[part]
+        for i in (0, 1):
+            row = SECOND + i * LATE if part else FIRST + i * EARLY
+            pair(k, i, row, n, 2 * (LATE if part else EARLY), at, n)
+        w = pl.ds(at, n)
+        remote(fs.at[k, c, w], fr.at[y, core, w], y_send.at[1], y_recv.at[k + part], device(x, y, zz, c)).start()
+        pltpu.make_async_copy(fs.at[k, core, w], fr.at[y, core, w], y_recv.at[k + part]).start()
 
     def chunk(t):
         landed(g.at[0, :, :, :, lanes(t, 0)], s2_recv.at[t, 0])
         landed(g.at[1, :, :, :, lanes(t, 1)], s2_recv.at[t, 1])
         project(t)
-        if t in READY:
-            pair(READY[t])
-            spread(READY[t])
 
     loads[0].wait()
+    pack_a(0, step(x, 2), s1a.at[step(x, 2)])
+    loads[1].wait()
+    pack_b(0, step(zz, 2), s1b.at[step(zz, 2)])
     pl.semaphore_wait(barrier, len(partners))
-    send_a(0, 2)
-    loads[1].wait()
-    send_b(0, 2)
+    first_copy(0, 0, 2).start()
+    first_copy(0, 1, 2).start()
     first_hop(0, True)
+    loads[2].wait()
     first_hop(1)
-    landed(bases_v, load_sem.at[2])
+    first_hop(2)
+    landed(bases_v, load_sem.at[3])
     bb[...] = jnp.zeros_like(bb)
     bb[0:RANK, :] = bases_v[0]
     bb[64 : 64 + RANK, :] = bases_v[0]
@@ -222,18 +239,25 @@
     for acc in (gxx, gxm, gyy, gym):
         acc[...] = jnp.zeros_like(acc)
     second_hop(0)
-    first_hop(2)
     second_hop(1)
+    first_hop(3)
+    second_hop(2)
     chunk(0)
-    second_hop(2)
-    first_hop(3)
+    chunk(1)
+    spread(0)
+    second_hop(3)
     first_hop(4)
-    chunk(1)
+    first_hop(5)
     chunk(2)
-    second_hop(3)
+    spread(1)
+    chunk(3)
+    spread(2)
     second_hop(4)
-    chunk(3)
+    second_hop(5)
     chunk(4)
+    swap(0)
+    chunk(5)
+    swap(1)
 
     eights = [(d, e) for d in range(4) for e in range(2)]
     sixteens = [(d, e) for d in (2, 1, 3, 0) for e in (2, 1, 3, 0)]
@@ -278,39 +302,40 @@
                 px, pc = step(x, d), lax.rem(core + e, 2)
                 remote(full.at[i, own_rows(x, core)], full.at[i, own_rows(x, core)], ag_send.at[i], ag_recv.at[i], device(px, y, zz, pc)).start()
 
-    wide = 5
-
-    def columns(u):
+    def columns(at, n):
         parts = []
-        for e in range(wide):
-            p = u * wide + e
+        for p in range(n):
             rows = []
             for s in range(4):
-                a, b = fr[s, 0, p], fr[s, 1, p]
+                a, b = fr[s, 0, at + p], fr[s, 1, at + p]
                 rows += [a[:JB], b[:JB], a[JB:], b[JB:]]
             parts.append(jnp.concatenate(rows, axis=0))
         return split(jnp.concatenate(parts, axis=1))
 
-    def gram(u, carry):
-        hi, lo = columns(u)
+    def gram(at, n):
+        hi, lo = columns(at, n)
         gyy[...] += dot(hi, hi, NT)
         gym[...] += dot(hi, lo, NT)
+
+    qhi, qlo = split(bq[...])
+    wide = 5
+
+    def finish(u, carry):
+        hi, lo = columns(u * wide, wide)
+        c = dot(qhi, hi, NN) + (dot(qlo, hi, NN) + dot(qhi, lo, NN))
+        for p in range(wide):
+            core_v[u * wide + p] = c[:, p * 128 : (p + 1) * 128]
         return carry
 
-    qhi, qlo = split(bq[...])
-
-    def finish(u, carry):
-        hi, lo = columns(u)
-        c = dot(qhi, hi, NN) + (dot(qlo, hi, NN) + dot(qhi, lo, NN))
-        for e in range(wide):
-            p = u * wide + e
-            core_v[p] = c[:, e * 128 : (e + 1) * 128]
-        return carry
-
-    for k in range(CHUNKS):
+    scatter(0, gxx, gxm, 1.0 / (MIDY * COLS))
+    for k in range(CHUNKS - 1):
         landed(fr.at[0], y_recv.at[k])
-    scatter(0, gxx, gxm, 1.0 / (MIDY * COLS))
-    lax.fori_loop(0, HP // wide, gram, 0)
+    landed(fr.at[0, :, 0:EP], y_recv.at[CHUNKS - 1])
+    gram(0, 6)
+    gram(6, 6)
+    gram(12, 5)
+    landed(fr.at[0, :, EP:HP], y_recv.at[CHUNKS])
+    gram(EP, LP)
     scatter(1, gyy, gym, 1.0 / (RANK * COLS))
     share(0)
     lax.fori_loop(0, HP // wide, finish, 0)
@@ -351,10 +376,12 @@
         ref[64:128, 128:192] = q1[:, :64]
         ref[128:192, 0:128] = jnp.where(left, t2[0:64], t0[64:128])
         ref[128:192, 128:192] = q2[:, :64]
+    odd = lax.rem(lax.axis_index("my"), 2)
     for p in range(HP):
         v = core[p]
-        core_out[p] = v[:RANK, :RANK]
-        core_out[p + HP] = pltpu.roll(v, 64, 1)[:RANK, :RANK]
+        first, gap = (LATE * odd + p, EP) if p < EP else (EARLY * (1 - odd) + p - EP, LP)
+        core_out[first] = v[:RANK, :RANK]
+        core_out[first + gap] = pltpu.roll(v, 64, 1)[:RANK, :RANK]
 
 
 def body(slab, basis_x, basis_y):
@@ -391,12 +418,12 @@
             pltpu.VMEM((2, 16, 24, 128), F32),
             pltpu.VMEM((2, 192, 128), F32),
             pltpu.VMEM((HP, 64, 128), F32),
-            pltpu.SemaphoreType.DMA((3,)),
+            pltpu.SemaphoreType.DMA((4,)),
             pltpu.SemaphoreType.DMA((4,)),
             pltpu.SemaphoreType.DMA((len(PARTS), 2)),
             pltpu.SemaphoreType.DMA((len(PARTS), 2)),
             pltpu.SemaphoreType.DMA((2,)),
-            pltpu.SemaphoreType.DMA((CHUNKS,)),
+            pltpu.SemaphoreType.DMA((CHUNKS + 1,)),
             pltpu.SemaphoreType.DMA((2,)),
             pltpu.SemaphoreType.DMA((2,)),
             pltpu.SemaphoreType.DMA((2,)),

time: 116 us -> 113 us (0.974)
  Pallas kernels: 115 us -> 112 us
    pallas_call x1, Pallas kernels: 112 us -> 109 us  [body(): pl.pallas_call(kernel, out_shape=(jax.ShapeDtypeStruct((2, 192, 128), F32...]
where the time goes in v4:
time: 113 us
  Pallas kernels  112 us (99%)
    pallas_call x1, Pallas kernels, body(): pl.pallas_call(kernel, out_shape=(jax.ShapeDtypeStruct((2, 192, 128), F32...  109 us
    pallas_call x1, Pallas kernels, body(): pl.pallas_call(unfold, out_shape=(jax.ShapeDtypeStruct((MIDX, MIDX), F32)...  2.82 us

profile of v4, /device:TPU:1, one launch (start us, length us, event | category | flops | bytes accessed | tf_op | source)
XLA Modules:
  0.0 112.8 jit_solution(7576228075807328686)
XLA Ops:
  0.6 109.3 %shard_map.58 = (f32[2,192,128]{2,1,0:T(8,128)}, f32[25,64,128]{2,1,0:T(8,128)}) custom-call(f32[12,24,6400]{2,1,0:T(8,128)} %bitcast.4, f32[60,192]{1,0:T(8,128)} %bitcast.5, f32[60,192]{1,0:T(8,128)} %bitcast.6), custom_call_target="tpu_custom_call" | custom-call | tf_op jit(solution)/shard_map/pallas_call | solution.py:390
  109.9 2.8 %shard_map.59 = (f32[192,192]{1,0:T(8,128)}, f32[192,192]{1,0:T(8,128)}, f32[50,60,60]{2,1,0:T(8,128)}) custom-call(f32[2,192,128]{2,1,0:T(8,128)} %get-tuple-element.8.full, f32[25,64,128]{2,1,0:T(8,128)} %get-tuple-element.9.core), custom_call_target="tpu_custom_call" | custom-call | tf_op jit(solution)/shard_map/pallas_call | solution.py:439

commit v5 on v4

--- a/solution.py
+++ b/solution.py
@@ -19,6 +19,7 @@
 PAIR = 2 * OWN
 HP = OWN // 2
 CHUNKS = 4
+AHEAD = (2, 1, 3, 0)
 EARLY, LATE = 34, 16
 EP, LP = EARLY // 2, LATE // 2
 RUNS = [(k * JB * PAIR + j * PAIR, k, j, 0, PAIR) for k in range(CHUNKS - 1) for j in range(JB)]
@@ -98,7 +99,7 @@
             if w >= count or at + size <= first * 128:
                 continue
             if k not in base:
-                base[k] = PAIR * ((lax.rem(pz, 2) * 4 + px) * 8 + step(y, 1 + k) * 2 + pz // 2)
+                base[k] = PAIR * ((lax.rem(pz, 2) * 4 + px) * 8 + step(y, AHEAD[k]) * 2 + pz // 2)
             off = base[k] + col
             t0 = off // 128
             t1 = jnp.minimum(t0 + 1, COLS // 128 - 1)
@@ -197,7 +198,7 @@
         lax.fori_loop(0, n, pairs, 0)
 
     def spread(k):
-        py = step(y, 1 + k)
+        py = step(y, AHEAD[k])
         for c in (0, 1):
             row = k * JB * PAIR + c * (OWN + LATE)
             pair(k, c, row, EP, PAIR, 0, EP)
@@ -207,17 +208,94 @@
     def swap(part):
         k, c = CHUNKS - 1, 1 - core
         at, n = ((0, EP), (EP, LP))[part]
-        for i in (0, 1):
+        w = pl.ds(at, n)
+
+        def collect(i):
             row = SECOND + i * LATE if part else FIRST + i * EARLY
             pair(k, i, row, n, 2 * (LATE if part else EARLY), at, n)
-        w = pl.ds(at, n)
+
+        collect(c)
         remote(fs.at[k, c, w], fr.at[y, core, w], y_send.at[1], y_recv.at[k + part], device(x, y, zz, c)).start()
+        collect(core)
         pltpu.make_async_copy(fs.at[k, core, w], fr.at[y, core, w], y_recv.at[k + part]).start()
 
     def chunk(t):
         landed(g.at[0, :, :, :, lanes(t, 0)], s2_recv.at[t, 0])
         landed(g.at[1, :, :, :, lanes(t, 1)], s2_recv.at[t, 1])
         project(t)
+
+    eights = [(d, e) for d in (2, 1, 3, 0) for e in (1, 0)]
+    sixteens = [(d, e) for d in (2, 1, 3, 0) for e in (2, 1, 3, 0)]
+    left = lax.broadcasted_iota(jnp.int32, (64, 128), 1) < 64
+
+    def own_rows(px, pc):
+        return pl.ds(pl.multiple_of((px * 2 + pc) * 24, 24), 24)
+
+    def scatter(i, main, cross, scale):
+        m = cross[...]
+        main[...] = (main[...] + (m + m.T)) * scale
+        part[i, 0:64] = main[0:64, 0:128]
+        high = jnp.concatenate([main[64:128, 128:192], jnp.zeros((64, 64), F32)], axis=1)
+        part[i, 64:128] = jnp.where(left, pltpu.roll(main[64:128, 0:128], 64, 1), pltpu.roll(high, 64, 1))
+        top = jnp.concatenate([main[0:64, 128:192], jnp.zeros((64, 64), F32)], axis=1)
+        end = jnp.concatenate([main[128:192, 128:192], jnp.zeros((64, 64), F32)], axis=1)
+        part[i, 128:192] = jnp.where(left, top, pltpu.roll(end, 64, 1))
+        for d, e in eights:
+            if d or e:
+                px, pc = step(x, d), lax.rem(core + e, 2)
+                remote(part.at[i, own_rows(px, pc)], parts8.at[i, d * 2 + e - 1], rs_send.at[i], rs_recv.at[i], device(px, y, zz, pc)).start()
+
+    def share(i):
+        landed(parts8.at[i], rs_recv.at[i])
+        total = part[i, own_rows(x, core)]
+        for n in range(7):
+            total += parts8[i, n]
+        sums[i] = total
+
+    def spread_yz(i):
+        parts16[i, y * 4 + zz] = sums[i]
+        for d, e in sixteens:
+            if d or e:
+                remote(sums.at[i], parts16.at[i, y * 4 + zz], bc_send.at[i], bc_recv.at[i], device(x, step(y, d), step(zz, e), core)).start()
+
+    def gather_yz(i):
+        landed(parts16.at[i, 0:15], bc_recv.at[i])
+        total = parts16[i, 0]
+        for n in range(1, 16):
+            total += parts16[i, n]
+        return total
+
+    def publish(i, total):
+        full[i, own_rows(x, core)] = total
+        for d, e in eights:
+            if d or e:
+                px, pc = step(x, d), lax.rem(core + e, 2)
+                remote(full.at[i, own_rows(x, core)], full.at[i, own_rows(x, core)], ag_send.at[i], ag_recv.at[i], device(px, y, zz, pc)).start()
+
+    def columns(at, n):
+        parts = []
+        for p in range(n):
+            rows = []
+            for s in range(4):
+                a, b = fr[s, 0, at + p], fr[s, 1, at + p]
+                rows += [a[:JB], b[:JB], a[JB:], b[JB:]]
+            parts.append(jnp.concatenate(rows, axis=0))
+        return split(jnp.concatenate(parts, axis=1))
+
+    def gram(at, n):
+        hi, lo = columns(at, n)
+        gyy[...] += dot(hi, hi, NT)
+        gym[...] += dot(hi, lo, NT)
+
+    wide = 5
+
+    def finish(u, carry):
+        qhi, qlo = split(bq[...])
+        hi, lo = columns(u * wide, wide)
+        c = dot(qhi, hi, NN) + (dot(qlo, hi, NN) + dot(qhi, lo, NN))
+        for p in range(wide):
+            core_v[u * wide + p] = c[:, p * 128 : (p + 1) * 128]
+        return carry
 
     loads[0].wait()
     pack_a(0, step(x, 2), s1a.at[step(x, 2)])
@@ -257,77 +335,9 @@
     chunk(4)
     swap(0)
     chunk(5)
+    scatter(0, gxx, gxm, 1.0 / (MIDY * COLS))
     swap(1)
 
-    eights = [(d, e) for d in range(4) for e in range(2)]
-    sixteens = [(d, e) for d in (2, 1, 3, 0) for e in (2, 1, 3, 0)]
-    left = lax.broadcasted_iota(jnp.int32, (64, 128), 1) < 64
-
-    def own_rows(px, pc):
-        return pl.ds(pl.multiple_of((px * 2 + pc) * 24, 24), 24)
-
-    def scatter(i, main, cross, scale):
-        m = cross[...]
-        main[...] = (main[...] + (m + m.T)) * scale
-        part[i, 0:64] = main[0:64, 0:128]
-        high = jnp.concatenate([main[64:128, 128:192], jnp.zeros((64, 64), F32)], axis=1)
-        part[i, 64:128] = jnp.where(left, pltpu.roll(main[64:128, 0:128], 64, 1), pltpu.roll(high, 64, 1))
-        top = jnp.concatenate([main[0:64, 128:192], jnp.zeros((64, 64), F32)], axis=1)
-        end = jnp.concatenate([main[128:192, 128:192], jnp.zeros((64, 64), F32)], axis=1)
-        part[i, 128:192] = jnp.where(left, top, pltpu.roll(end, 64, 1))
-        for d, e in eights[::-1]:
-            if d or e:
-                px, pc = step(x, d), lax.rem(core + e, 2)
-                remote(part.at[i, own_rows(px, pc)], parts8.at[i, d * 2 + e - 1], rs_send.at[i], rs_recv.at[i], device(px, y, zz, pc)).start()
-
-    def share(i):
-        landed(parts8.at[i], rs_recv.at[i])
-        total = part[i, own_rows(x, core)]
-        for n in range(7):
-            total += parts8[i, n]
-        sums[i] = total
-        for d, e in sixteens:
-            if d or e:
-                remote(sums.at[i], parts16.at[i, y * 4 + zz], bc_send.at[i], bc_recv.at[i], device(x, step(y, d), step(zz, e), core)).start()
-        parts16[i, y * 4 + zz] = total
-
-    def gather(i):
-        landed(parts16.at[i, 0:15], bc_recv.at[i])
-        total = parts16[i, 0]
-        for n in range(1, 16):
-            total += parts16[i, n]
-        full[i, own_rows(x, core)] = total
-        for d, e in eights[::-1]:
-            if d or e:
-                px, pc = step(x, d), lax.rem(core + e, 2)
-                remote(full.at[i, own_rows(x, core)], full.at[i, own_rows(x, core)], ag_send.at[i], ag_recv.at[i], device(px, y, zz, pc)).start()
-
-    def columns(at, n):
-        parts = []
-        for p in range(n):
-            rows = []
-            for s in range(4):
-                a, b = fr[s, 0, at + p], fr[s, 1, at + p]
-                rows += [a[:JB], b[:JB], a[JB:], b[JB:]]
-            parts.append(jnp.concatenate(rows, axis=0))
-        return split(jnp.concatenate(parts, axis=1))
-
-    def gram(at, n):
-        hi, lo = columns(at, n)
-        gyy[...] += dot(hi, hi, NT)
-        gym[...] += dot(hi, lo, NT)
-
-    qhi, qlo = split(bq[...])
-    wide = 5
-
-    def finish(u, carry):
-        hi, lo = columns(u * wide, wide)
-        c = dot(qhi, hi, NN) + (dot(qlo, hi, NN) + dot(qhi, lo, NN))
-        for p in range(wide):
-            core_v[u * wide + p] = c[:, p * 128 : (p + 1) * 128]
-        return carry
-
-    scatter(0, gxx, gxm, 1.0 / (MIDY * COLS))
     for k in range(CHUNKS - 1):
         landed(fr.at[0], y_recv.at[k])
     landed(fr.at[0, :, 0:EP], y_recv.at[CHUNKS - 1])
@@ -338,12 +348,14 @@
     gram(EP, LP)
     scatter(1, gyy, gym, 1.0 / (RANK * COLS))
     share(0)
+    spread_yz(0)
+    share(1)
+    spread_yz(1)
     lax.fori_loop(0, HP // wide, finish, 0)
     core_store = pltpu.make_async_copy(core_v, core_out, store_sem.at[0])
     core_store.start()
-    share(1)
-    gather(0)
-    gather(1)
+    publish(0, gather_yz(0))
+    publish(1, gather_yz(1))
     landed(s1a.at[0:3], hop_send.at[0])
     landed(s1b.at[0:3], hop_send.at[1])
     landed(r1a.at[0:3], hop_send.at[2])

time: 113 us -> 112 us (level)
  no operation moved by 1% of the time
where the time goes in v5:
time: 112 us
  Pallas kernels  111 us (99%)
    pallas_call x1, Pallas kernels, body(): pl.pallas_call(kernel, out_shape=(jax.ShapeDtypeStruct((2, 192, 128), F32...  109 us
    pallas_call x1, Pallas kernels, body(): pl.pallas_call(unfold, out_shape=(jax.ShapeDtypeStruct((MIDX, MIDX), F32)...  2.82 us

profile of v5, /device:TPU:1, one launch (start us, length us, event | category | flops | bytes accessed | tf_op | source)
XLA Modules:
  0.0 112.0 jit_solution(13903954941472744742)
XLA Ops:
  0.6 108.6 %shard_map.58 = (f32[2,192,128]{2,1,0:T(8,128)}, f32[25,64,128]{2,1,0:T(8,128)}) custom-call(f32[12,24,6400]{2,1,0:T(8,128)} %bitcast.4, f32[60,192]{1,0:T(8,128)} %bitcast.5, f32[60,192]{1,0:T(8,128)} %bitcast.6), custom_call_target="tpu_custom_call" | custom-call | tf_op jit(solution)/shard_map/pallas_call | solution.py:402
  109.2 2.8 %shard_map.59 = (f32[192,192]{1,0:T(8,128)}, f32[192,192]{1,0:T(8,128)}, f32[50,60,60]{2,1,0:T(8,128)}) custom-call(f32[2,192,128]{2,1,0:T(8,128)} %get-tuple-element.8.full, f32[25,64,128]{2,1,0:T(8,128)} %get-tuple-element.9.core), custom_call_target="tpu_custom_call" | custom-call | tf_op jit(solution)/shard_map/pallas_call | solution.py:451

commit v6 on v5

--- a/solution.py
+++ b/solution.py
@@ -179,8 +179,9 @@
             hi, lo = split(jnp.concatenate(blocks, axis=1))
             gxx[...] += dot(hi, hi, NT)
             gxm[...] += dot(hi, lo, NT)
-            bhi, blo = split(bb[...])
-            f = dot(bhi, hi, NN) + (dot(blo, hi, NN) + dot(bhi, lo, NN))
+            f = dot(bb[...], hi, NN)
+            f = f[0:64] + (f[64:128] + dot(bb[0:64], lo, NN))
+            f = jnp.concatenate([f, f], axis=0)
             at = 0
             for h, v in group:
                 first, size = PARTS[t][h][0] * 128, PARTS[t][h][1] * 128
@@ -195,7 +196,7 @@
                 fs[k, c, at + p, v * JB : (v + 1) * JB, :] = jnp.where(low, a, b)
             return carry
 
-        lax.fori_loop(0, n, pairs, 0)
+        lax.fori_loop(0, n, pairs, 0, unroll=True)
 
     def spread(k):
         py = step(y, AHEAD[k])
@@ -290,9 +291,9 @@
     wide = 5
 
     def finish(u, carry):
-        qhi, qlo = split(bq[...])
         hi, lo = columns(u * wide, wide)
-        c = dot(qhi, hi, NN) + (dot(qlo, hi, NN) + dot(qhi, lo, NN))
+        c = dot(bq[...], hi, NN)
+        c = c[0:64] + (c[64:128] + dot(bq[0:64], lo, NN))
         for p in range(wide):
             core_v[u * wide + p] = c[:, p * 128 : (p + 1) * 128]
         return carry
@@ -309,11 +310,10 @@
     first_hop(1)
     first_hop(2)
     landed(bases_v, load_sem.at[3])
-    bb[...] = jnp.zeros_like(bb)
-    bb[0:RANK, :] = bases_v[0]
-    bb[64 : 64 + RANK, :] = bases_v[0]
-    bq[...] = jnp.zeros_like(bq)
-    bq[0:RANK, :] = bases_v[1]
+    for n, ref in enumerate((bb, bq)):
+        hi, lo = split(jnp.concatenate([bases_v[n], jnp.zeros((64 - RANK, MIDX), F32)], axis=0))
+        ref[0:64] = hi
+        ref[64:128] = lo
     for acc in (gxx, gxm, gyy, gym):
         acc[...] = jnp.zeros_like(acc)
     second_hop(0)
@@ -418,8 +418,8 @@
             pltpu.VMEM((CHUNKS, 2, HP, 2 * JB, 128), F32),
             pltpu.VMEM((4, 2, HP, 2 * JB, 128), F32),
             pltpu.VMEM((2, RANK, MIDX), F32),
-            pltpu.VMEM((128, MIDX), F32),
-            pltpu.VMEM((64, MIDY), F32),
+            pltpu.VMEM((128, MIDX), BF16),
+            pltpu.VMEM((128, MIDY), BF16),
             pltpu.VMEM((MIDX, MIDX), F32),
             pltpu.VMEM((MIDX, MIDX), F32),
             pltpu.VMEM((MIDY, MIDY), F32),

time: 112 us -> 112 us (level)
  no operation moved by 1% of the time
where the time goes in v6:
time: 112 us
  Pallas kernels  111 us (99%)
    pallas_call x1, Pallas kernels, body(): pl.pallas_call(kernel, out_shape=(jax.ShapeDtypeStruct((2, 192, 128), F32...  108 us
    pallas_call x1, Pallas kernels, body(): pl.pallas_call(unfold, out_shape=(jax.ShapeDtypeStruct((MIDX, MIDX), F32)...  2.82 us

profile of v6, /device:TPU:1, one launch (start us, length us, event | category | flops | bytes accessed | tf_op | source)
XLA Modules:
  0.0 111.7 jit_solution(9116706411893152659)
XLA Ops:
  0.6 108.3 %shard_map.58 = (f32[2,192,128]{2,1,0:T(8,128)}, f32[25,64,128]{2,1,0:T(8,128)}) custom-call(f32[12,24,6400]{2,1,0:T(8,128)} %bitcast.4, f32[60,192]{1,0:T(8,128)} %bitcast.5, f32[60,192]{1,0:T(8,128)} %bitcast.6), custom_call_target="tpu_custom_call" | custom-call | tf_op jit(solution)/shard_map/pallas_call | solution.py:402
  108.9 2.8 %shard_map.59 = (f32[192,192]{1,0:T(8,128)}, f32[192,192]{1,0:T(8,128)}, f32[50,60,60]{2,1,0:T(8,128)}) custom-call(f32[2,192,128]{2,1,0:T(8,128)} %get-tuple-element.8.full, f32[25,64,128]{2,1,0:T(8,128)} %get-tuple-element.9.core), custom_call_target="tpu_custom_call" | custom-call | tf_op jit(solution)/shard_map/pallas_call | solution.py:451

commit v7 on v6

--- a/solution.py
+++ b/solution.py
@@ -52,9 +52,9 @@
 def kernel(
     slab, bxt, byt, full_out, core_out,
     raw, s1a, s1b, r1a, r1b, g, ft, fs, fr, bases_v, bb, bq, gxx, gxm, gyy, gym,
-    part, parts8, sums, parts16, full, core_v,
+    part, parts8, sums, parts16, done, core_v,
     load_sem, hop_send, s1_recv, s2_recv, y_send, y_recv, store_sem,
-    rs_send, rs_recv, bc_send, bc_recv, ag_send, ag_recv,
+    sum_send, rs_recv, bc_recv, ag_recv,
 ):
     mx, my = lax.axis_index("mx"), lax.axis_index("my")
     x, zh = lax.rem(mx, 4), mx // 4
@@ -89,6 +89,9 @@
 
     def lanes(t, h):
         return pl.ds(STARTS[t][h] * 128, PARTS[t][h][1] * 128)
+
+    def whole(t):
+        return pl.ds(0, (PARTS[t][0][1] + PARTS[t][1][1]) * 128)
 
     def pack(t, h, px, pz, dst):
         first, count = PARTS[t][h]
@@ -134,9 +137,9 @@
         w = lanes(t, h)
         if h == 0:
             px = step(x, d)
-            return remote(s1a.at[px, :, :, w], r1a.at[x, :, :, w], hop_send.at[0], s1_recv.at[t, 0], device(px, y, zz, core))
+            return remote(s1a.at[px, :, :, w], r1a.at[x, :, :, w], hop_send.at[0], s1_recv.at[t], device(px, y, zz, core))
         pz = step(zz, d)
-        return remote(s1b.at[pz, :, :, w], r1b.at[zz, :, :, w], hop_send.at[1], s1_recv.at[t, 1], device(x, y, pz, core))
+        return remote(s1b.at[pz, :, :, w], r1b.at[zz, :, :, w], hop_send.at[0], s1_recv.at[t], device(x, y, pz, core))
 
     def send_a(t, d):
         px = step(x, d)
@@ -161,14 +164,13 @@
 
     def second_hop(t):
         wa, wb = lanes(t, 0), lanes(t, 1)
-        landed(r1a.at[0:3, :, :, wa], s1_recv.at[t, 0])
-        landed(r1b.at[0:3, :, :, wb], s1_recv.at[t, 1])
+        landed(r1a.at[0:3, :, :, whole(t)], s1_recv.at[t])
         for d in (2, 1, 3):
             px, pz = step(x, d), step(zz, d)
-            remote(r1a.at[:, pz, :, wa], g.at[0, zz, :, :, wa], hop_send.at[2], s2_recv.at[t, 0], device(x, y, pz, core)).start()
-            remote(r1b.at[:, px, :, wb], g.at[1, :, x, :, wb], hop_send.at[3], s2_recv.at[t, 1], device(px, y, zz, core)).start()
-        pltpu.make_async_copy(r1a.at[:, zz, :, wa], g.at[0, zz, :, :, wa], s2_recv.at[t, 0]).start()
-        pltpu.make_async_copy(r1b.at[:, x, :, wb], g.at[1, :, x, :, wb], s2_recv.at[t, 1]).start()
+            remote(r1a.at[:, pz, :, wa], g.at[0, zz, :, :, wa], hop_send.at[1], s2_recv.at[t], device(x, y, pz, core)).start()
+            remote(r1b.at[:, px, :, wb], g.at[1, :, x, :, wb], hop_send.at[1], s2_recv.at[t], device(px, y, zz, core)).start()
+        pltpu.make_async_copy(r1a.at[:, zz, :, wa], g.at[0, zz, :, :, wa], s2_recv.at[t]).start()
+        pltpu.make_async_copy(r1b.at[:, x, :, wb], g.at[1, :, x, :, wb], s2_recv.at[t]).start()
 
     low = lax.broadcasted_iota(jnp.int32, (JB, 128), 1) < 64
 
@@ -204,7 +206,7 @@
             row = k * JB * PAIR + c * (OWN + LATE)
             pair(k, c, row, EP, PAIR, 0, EP)
             pair(k, c, k * JB * PAIR + (OWN if c else EARLY), LP, PAIR, EP, LP)
-            remote(fs.at[k, c], fr.at[y, core], y_send.at[0], y_recv.at[k], device(x, py, zz, c)).start()
+            remote(fs.at[k, c], fr.at[y, core], y_send, y_recv.at[k], device(x, py, zz, c)).start()
 
     def swap(part):
         k, c = CHUNKS - 1, 1 - core
@@ -216,13 +218,12 @@
             pair(k, i, row, n, 2 * (LATE if part else EARLY), at, n)
 
         collect(c)
-        remote(fs.at[k, c, w], fr.at[y, core, w], y_send.at[1], y_recv.at[k + part], device(x, y, zz, c)).start()
+        remote(fs.at[k, c, w], fr.at[y, core, w], y_send, y_recv.at[k + part], device(x, y, zz, c)).start()
         collect(core)
         pltpu.make_async_copy(fs.at[k, core, w], fr.at[y, core, w], y_recv.at[k + part]).start()
 
     def chunk(t):
-        landed(g.at[0, :, :, :, lanes(t, 0)], s2_recv.at[t, 0])
-        landed(g.at[1, :, :, :, lanes(t, 1)], s2_recv.at[t, 1])
+        landed(g.at[0, :, :, :, whole(t)], s2_recv.at[t])
         project(t)
 
     eights = [(d, e) for d in (2, 1, 3, 0) for e in (1, 0)]
@@ -244,7 +245,7 @@
         for d, e in eights:
             if d or e:
                 px, pc = step(x, d), lax.rem(core + e, 2)
-                remote(part.at[i, own_rows(px, pc)], parts8.at[i, d * 2 + e - 1], rs_send.at[i], rs_recv.at[i], device(px, y, zz, pc)).start()
+                remote(part.at[i, own_rows(px, pc)], parts8.at[i, d * 2 + e - 1], sum_send, rs_recv.at[i], device(px, y, zz, pc)).start()
 
     def share(i):
         landed(parts8.at[i], rs_recv.at[i])
@@ -257,7 +258,7 @@
         parts16[i, y * 4 + zz] = sums[i]
         for d, e in sixteens:
             if d or e:
-                remote(sums.at[i], parts16.at[i, y * 4 + zz], bc_send.at[i], bc_recv.at[i], device(x, step(y, d), step(zz, e), core)).start()
+                remote(sums.at[i], parts16.at[i, y * 4 + zz], sum_send, bc_recv.at[i], device(x, step(y, d), step(zz, e), core)).start()
 
     def gather_yz(i):
         landed(parts16.at[i, 0:15], bc_recv.at[i])
@@ -267,11 +268,13 @@
         return total
 
     def publish(i, total):
-        full[i, own_rows(x, core)] = total
+        done[i] = total
+        mine = full_out.at[i, own_rows(x, core)]
         for d, e in eights:
             if d or e:
                 px, pc = step(x, d), lax.rem(core + e, 2)
-                remote(full.at[i, own_rows(x, core)], full.at[i, own_rows(x, core)], ag_send.at[i], ag_recv.at[i], device(px, y, zz, pc)).start()
+                remote(done.at[i], mine, sum_send, ag_recv.at[i], device(px, y, zz, pc)).start()
+        pltpu.make_async_copy(done.at[i], mine, ag_recv.at[i]).start()
 
     def columns(at, n):
         parts = []
@@ -352,27 +355,17 @@
     share(1)
     spread_yz(1)
     lax.fori_loop(0, HP // wide, finish, 0)
-    core_store = pltpu.make_async_copy(core_v, core_out, store_sem.at[0])
+    core_store = pltpu.make_async_copy(core_v, core_out, store_sem)
     core_store.start()
     publish(0, gather_yz(0))
     publish(1, gather_yz(1))
-    landed(s1a.at[0:3], hop_send.at[0])
-    landed(s1b.at[0:3], hop_send.at[1])
-    landed(r1a.at[0:3], hop_send.at[2])
-    landed(r1b.at[0:3], hop_send.at[3])
-    landed(fs.at[0:3], y_send.at[0])
-    landed(fs.at[3, 0], y_send.at[1])
-    for i in (0, 1):
-        landed(parts8.at[i], rs_send.at[i])
-        landed(parts16.at[i, 0:15], bc_send.at[i])
+    landed(g.at[:, 0:3], hop_send.at[0])
+    landed(g.at[:, 0:3], hop_send.at[1])
+    landed(ft.at[0, 0 : 7 * HP * 2 * JB], y_send)
     core_store.wait()
     for i in (0, 1):
-        landed(full.at[i, 0:168], ag_recv.at[i])
-    store = pltpu.make_async_copy(full, full_out, store_sem.at[1])
-    store.start()
-    for i in (0, 1):
-        landed(full.at[i, 0:168], ag_send.at[i])
-    store.wait()
+        landed(full_out.at[i], ag_recv.at[i])
+    landed(ft.at[0, 0 : 2 * (7 + 15 + 7) * 24], sum_send)
 
 
 def unfold(full, core, gx_out, gy_out, core_out):
@@ -428,18 +421,16 @@
             pltpu.VMEM((2, 7, 24, 128), F32),
             pltpu.VMEM((2, 24, 128), F32),
             pltpu.VMEM((2, 16, 24, 128), F32),
-            pltpu.VMEM((2, 192, 128), F32),
+            pltpu.VMEM((2, 24, 128), F32),
             pltpu.VMEM((HP, 64, 128), F32),
             pltpu.SemaphoreType.DMA((4,)),
-            pltpu.SemaphoreType.DMA((4,)),
-            pltpu.SemaphoreType.DMA((len(PARTS), 2)),
-            pltpu.SemaphoreType.DMA((len(PARTS), 2)),
             pltpu.SemaphoreType.DMA((2,)),
+            pltpu.SemaphoreType.DMA((len(PARTS),)),
+            pltpu.SemaphoreType.DMA((len(PARTS),)),
+            pltpu.SemaphoreType.DMA,
             pltpu.SemaphoreType.DMA((CHUNKS + 1,)),
-            pltpu.SemaphoreType.DMA((2,)),
-            pltpu.SemaphoreType.DMA((2,)),
-            pltpu.SemaphoreType.DMA((2,)),
-            pltpu.SemaphoreType.DMA((2,)),
+            pltpu.SemaphoreType.DMA,
+            pltpu.SemaphoreType.DMA,
             pltpu.SemaphoreType.DMA((2,)),
             pltpu.SemaphoreType.DMA((2,)),
             pltpu.SemaphoreType.DMA((2,)),

time: 112 us -> 111 us (level)
  no operation moved by 1% of the time
where the time goes in v7:
time: 111 us
  Pallas kernels  110 us (99%)
    pallas_call x1, Pallas kernels, body(): pl.pallas_call(kernel, out_shape=(jax.ShapeDtypeStruct((2, 192, 128), F32...  107 us
    pallas_call x1, Pallas kernels, body(): pl.pallas_call(unfold, out_shape=(jax.ShapeDtypeStruct((MIDX, MIDX), F32)...  2.82 us

profile of v7, /device:TPU:1, one launch (start us, length us, event | category | flops | bytes accessed | tf_op | source)
XLA Modules:
  0.0 111.0 jit_solution(10576608390055879469)
XLA Ops:
  0.6 107.5 %shard_map.58 = (f32[2,192,128]{2,1,0:T(8,128)}, f32[25,64,128]{2,1,0:T(8,128)}) custom-call(f32[12,24,6400]{2,1,0:T(8,128)} %bitcast.4, f32[60,192]{1,0:T(8,128)} %bitcast.5, f32[60,192]{1,0:T(8,128)} %bitcast.6), custom_call_target="tpu_custom_call" | custom-call | tf_op jit(solution)/shard_map/pallas_call | solution.py:395
  108.1 2.8 %shard_map.59 = (f32[192,192]{1,0:T(8,128)}, f32[192,192]{1,0:T(8,128)}, f32[50,60,60]{2,1,0:T(8,128)}) custom-call(f32[2,192,128]{2,1,0:T(8,128)} %get-tuple-element.8.full, f32[25,64,128]{2,1,0:T(8,128)} %get-tuple-element.9.core), custom_call_target="tpu_custom_call" | custom-call | tf_op jit(solution)/shard_map/pallas_call | solution.py:442

commit v8 on v7

--- a/solution.py
+++ b/solution.py
@@ -34,6 +34,7 @@
 )
 TILES = 38
 LANES = TILES // 2 * 128
+FOLDED = 4
 STARTS = ((0, 0), (2, 2), (5, 5), (10, 10), (15, 14), (18, 17))
 
 NT = (((1,), (1,)), ((), ()))
@@ -51,9 +52,9 @@
 
 def kernel(
     slab, bxt, byt, full_out, core_out,
-    raw, s1a, s1b, r1a, r1b, g, ft, fs, fr, bases_v, bb, bq, gxx, gxm, gyy, gym,
+    raw, s1a, s1b, r1a, r1b, g, s1f, r1f, s2f, gf, ft, fs, fr, bases_v, bb, bq, gxx, gxm, gyy, gym,
     part, parts8, sums, parts16, done, core_v,
-    load_sem, hop_send, s1_recv, s2_recv, y_send, y_recv, store_sem,
+    load_sem, hop_send, fold_sem, s1_recv, s2_recv, y_send, y_recv, store_sem,
     sum_send, rs_recv, bc_recv, ag_recv,
 ):
     mx, my = lax.axis_index("mx"), lax.axis_index("my")
@@ -87,11 +88,27 @@
 
     lane = lax.broadcasted_iota(jnp.int32, (IB, 128), 1)
 
+    def held(t, h):
+        return pl.ds(STARTS[t][h] * 128, PARTS[t][h][1] * 128)
+
+    def tiles_sent(t, h):
+        return PARTS[t][h][1] - ((t, h) == (FOLDED, 1))
+
     def lanes(t, h):
-        return pl.ds(STARTS[t][h] * 128, PARTS[t][h][1] * 128)
+        return pl.ds(STARTS[t][h] * 128, tiles_sent(t, h) * 128)
+
+    fold_tile = pl.ds((STARTS[FOLDED][1] + tiles_sent(FOLDED, 1)) * 128, 128)
+    half = lane < 64
+
+    def joined(a, b):
+        return jnp.where(half, a, pltpu.roll(b, 64, 1))
+
+    def fold(blocks, dst):
+        for n in (0, 1):
+            dst[n] = joined(blocks[2 * n, :, fold_tile], blocks[2 * n + 1, :, fold_tile])
 
     def whole(t):
-        return pl.ds(0, (PARTS[t][0][1] + PARTS[t][1][1]) * 128)
+        return pl.ds(0, (tiles_sent(t, 0) + tiles_sent(t, 1)) * 128)
 
     def pack(t, h, px, pz, dst):
         first, count = PARTS[t][h]
@@ -150,6 +167,9 @@
         pz = step(zz, d)
         pack_b(t, pz, s1b.at[pz])
         first_copy(t, 1, d).start()
+        if t == FOLDED:
+            fold(s1b.at[pz], s1f.at[pz])
+            remote(s1f.at[pz], r1f.at[zz], fold_sem.at[0], fold_sem.at[1], device(x, y, pz, core)).start()
 
     def first_hop(t, begun=False):
         def message(n, carry):
@@ -161,6 +181,8 @@
         lax.fori_loop(1 if begun else 0, 3, message, 0)
         pack_a(t, x, r1a.at[x])
         pack_b(t, zz, r1b.at[zz])
+        if t == FOLDED:
+            fold(r1b.at[zz], r1f.at[zz])
 
     def second_hop(t):
         wa, wb = lanes(t, 0), lanes(t, 1)
@@ -169,6 +191,16 @@
             px, pz = step(x, d), step(zz, d)
             remote(r1a.at[:, pz, :, wa], g.at[0, zz, :, :, wa], hop_send.at[1], s2_recv.at[t], device(x, y, pz, core)).start()
             remote(r1b.at[:, px, :, wb], g.at[1, :, x, :, wb], hop_send.at[1], s2_recv.at[t], device(px, y, zz, core)).start()
+        if t == FOLDED:
+            landed(r1f.at[0:3], fold_sem.at[1])
+            for px in range(4):
+                for n in (0, 1):
+                    a, b = r1f[2 * n, px // 2], r1f[2 * n + 1, px // 2]
+                    s2f[px, n] = joined(a, b) if px % 2 == 0 else jnp.where(half, pltpu.roll(a, 64, 1), b)
+            for d in (2, 1, 3):
+                px = step(x, d)
+                remote(s2f.at[px], gf.at[x], fold_sem.at[0], fold_sem.at[2], device(px, y, zz, core)).start()
+            gf[x] = s2f[x]
         pltpu.make_async_copy(r1a.at[:, zz, :, wa], g.at[0, zz, :, :, wa], s2_recv.at[t]).start()
         pltpu.make_async_copy(r1b.at[:, x, :, wb], g.at[1, :, x, :, wb], s2_recv.at[t]).start()
 
@@ -177,7 +209,7 @@
     def project(t):
         both = [(h, v) for h in (0, 1) for v in (0, 1)]
         for group in (both,) if t > 3 else (both[:2], both[2:]):
-            blocks = [g[h, v * 2 : v * 2 + 2, :, :, lanes(t, h)].reshape(MIDX, -1) for h, v in group]
+            blocks = [g[h, v * 2 : v * 2 + 2, :, :, held(t, h)].reshape(MIDX, -1) for h, v in group]
             hi, lo = split(jnp.concatenate(blocks, axis=1))
             gxx[...] += dot(hi, hi, NT)
             gxm[...] += dot(hi, lo, NT)
@@ -224,6 +256,13 @@
 
     def chunk(t):
         landed(g.at[0, :, :, :, whole(t)], s2_recv.at[t])
+        if t == FOLDED:
+            landed(gf.at[0:3], fold_sem.at[2])
+            for v in (0, 1):
+                for px in range(4):
+                    both = gf[px, v]
+                    g[1, 2 * v, px, :, fold_tile] = jnp.where(half, both, 0.0)
+                    g[1, 2 * v + 1, px, :, fold_tile] = jnp.where(half, pltpu.roll(both, 64, 1), 0.0)
         project(t)
 
     eights = [(d, e) for d in (2, 1, 3, 0) for e in (1, 0)]
@@ -359,8 +398,10 @@
     core_store.start()
     publish(0, gather_yz(0))
     publish(1, gather_yz(1))
-    landed(g.at[:, 0:3], hop_send.at[0])
-    landed(g.at[:, 0:3], hop_send.at[1])
+    for hop in (0, 1):
+        landed(g.at[0, 0:3], hop_send.at[hop])
+        landed(g.at[0, 0:3, :, :, 0 : LANES - 128], hop_send.at[hop])
+    landed(ft.at[0, 0 : 6 * 2 * IB], fold_sem.at[0])
     landed(ft.at[0, 0 : 7 * HP * 2 * JB], y_send)
     core_store.wait()
     for i in (0, 1):
@@ -407,6 +448,10 @@
             pltpu.VMEM((4, 4, IB, LANES), F32),
             pltpu.VMEM((4, 4, IB, LANES), F32),
             pltpu.VMEM((2, 4, 4, IB, LANES), F32),
+            pltpu.VMEM((4, 2, IB, 128), F32),
+            pltpu.VMEM((4, 2, IB, 128), F32),
+            pltpu.VMEM((4, 2, IB, 128), F32),
+            pltpu.VMEM((4, 2, IB, 128), F32),
             pltpu.VMEM((2, TILES * 128, 128), F32),
             pltpu.VMEM((CHUNKS, 2, HP, 2 * JB, 128), F32),
             pltpu.VMEM((4, 2, HP, 2 * JB, 128), F32),
@@ -425,6 +470,7 @@
             pltpu.VMEM((HP, 64, 128), F32),
             pltpu.SemaphoreType.DMA((4,)),
             pltpu.SemaphoreType.DMA((2,)),
+            pltpu.SemaphoreType.DMA((3,)),
             pltpu.SemaphoreType.DMA((len(PARTS),)),
             pltpu.SemaphoreType.DMA((len(PARTS),)),
             pltpu.SemaphoreType.DMA,

time: 111 us -> 110 us (level)
    pallas_call x1, Pallas kernels: 107 us -> 106 us  [body(): pl.pallas_call(kernel, out_shape=(jax.ShapeDtypeStruct((2, 192, 128), F32...]
where the time goes in v8:
time: 110 us
  Pallas kernels  109 us (99%)
    pallas_call x1, Pallas kernels, body(): pl.pallas_call(kernel, out_shape=(jax.ShapeDtypeStruct((2, 192, 128), F32...  106 us
    pallas_call x1, Pallas kernels, body(): pl.pallas_call(unfold, out_shape=(jax.ShapeDtypeStruct((MIDX, MIDX), F32)...  2.82 us

profile of v8, /device:TPU:1, one launch (start us, length us, event | category | flops | bytes accessed | tf_op | source)
XLA Modules:
  0.0 109.7 jit_solution(6264678518658357245)
XLA Ops:
  0.6 106.3 %shard_map.58 = (f32[2,192,128]{2,1,0:T(8,128)}, f32[25,64,128]{2,1,0:T(8,128)}) custom-call(f32[12,24,6400]{2,1,0:T(8,128)} %bitcast.4, f32[60,192]{1,0:T(8,128)} %bitcast.5, f32[60,192]{1,0:T(8,128)} %bitcast.6), custom_call_target="tpu_custom_call" | custom-call | tf_op jit(solution)/shard_map/pallas_call | solution.py:436
  106.9 2.8 %shard_map.59 = (f32[192,192]{1,0:T(8,128)}, f32[192,192]{1,0:T(8,128)}, f32[50,60,60]{2,1,0:T(8,128)}) custom-call(f32[2,192,128]{2,1,0:T(8,128)} %get-tuple-element.8.full, f32[25,64,128]{2,1,0:T(8,128)} %get-tuple-element.9.core), custom_call_target="tpu_custom_call" | custom-call | tf_op jit(solution)/shard_map/pallas_call | solution.py:488

commit v9 on v8

--- a/solution.py
+++ b/solution.py
@@ -266,7 +266,8 @@
         project(t)
 
     eights = [(d, e) for d in (2, 1, 3, 0) for e in (1, 0)]
-    sixteens = [(d, e) for d in (2, 1, 3, 0) for e in (2, 1, 3, 0)]
+    sixteens = [(2, 2), (2, 1), (1, 2), (2, 3), (3, 2), (1, 1), (3, 3), (1, 3), (3, 1)]
+    sixteens += [(0, 2), (2, 0), (0, 1), (1, 0), (0, 3), (3, 0), (0, 0)]
     left = lax.broadcasted_iota(jnp.int32, (64, 128), 1) < 64
 
     def own_rows(px, pc):

time: 110 us -> 110 us (level)
  no operation moved by 1% of the time
where the time goes in v9:
time: 110 us
  Pallas kernels  109 us (99%)
    pallas_call x1, Pallas kernels, body(): pl.pallas_call(kernel, out_shape=(jax.ShapeDtypeStruct((2, 192, 128), F32...  106 us
    pallas_call x1, Pallas kernels, body(): pl.pallas_call(unfold, out_shape=(jax.ShapeDtypeStruct((MIDX, MIDX), F32)...  2.82 us

profile of v9, /device:TPU:1, one launch (start us, length us, event | category | flops | bytes accessed | tf_op | source)
XLA Modules:
  0.0 109.7 jit_solution(1927185213175269680)
XLA Ops:
  0.6 106.3 %shard_map.58 = (f32[2,192,128]{2,1,0:T(8,128)}, f32[25,64,128]{2,1,0:T(8,128)}) custom-call(f32[12,24,6400]{2,1,0:T(8,128)} %bitcast.4, f32[60,192]{1,0:T(8,128)} %bitcast.5, f32[60,192]{1,0:T(8,128)} %bitcast.6), custom_call_target="tpu_custom_call" | custom-call | tf_op jit(solution)/shard_map/pallas_call | solution.py:437
  106.9 2.8 %shard_map.59 = (f32[192,192]{1,0:T(8,128)}, f32[192,192]{1,0:T(8,128)}, f32[50,60,60]{2,1,0:T(8,128)}) custom-call(f32[2,192,128]{2,1,0:T(8,128)} %get-tuple-element.8.full, f32[25,64,128]{2,1,0:T(8,128)} %get-tuple-element.9.core), custom_call_target="tpu_custom_call" | custom-call | tf_op jit(solution)/shard_map/pallas_call | solution.py:489

commit v10 on v9

--- a/solution.py
+++ b/solution.py
@@ -265,7 +265,7 @@
                     g[1, 2 * v + 1, px, :, fold_tile] = jnp.where(half, pltpu.roll(both, 64, 1), 0.0)
         project(t)
 
-    eights = [(d, e) for d in (2, 1, 3, 0) for e in (1, 0)]
+    eights = [(2, 1), (2, 0), (1, 1), (3, 1), (1, 0), (3, 0), (0, 1), (0, 0)]
     sixteens = [(2, 2), (2, 1), (1, 2), (2, 3), (3, 2), (1, 1), (3, 3), (1, 3), (3, 1)]
     sixteens += [(0, 2), (2, 0), (0, 1), (1, 0), (0, 3), (3, 0), (0, 0)]
     left = lax.broadcasted_iota(jnp.int32, (64, 128), 1) < 64

time: 110 us -> 110 us (level)
  no operation moved by 1% of the time
where the time goes in v10:
time: 110 us
  Pallas kernels  109 us (99%)
    pallas_call x1, Pallas kernels, body(): pl.pallas_call(kernel, out_shape=(jax.ShapeDtypeStruct((2, 192, 128), F32...  106 us
    pallas_call x1, Pallas kernels, body(): pl.pallas_call(unfold, out_shape=(jax.ShapeDtypeStruct((MIDX, MIDX), F32)...  2.82 us

profile of v10, /device:TPU:1, one launch (start us, length us, event | category | flops | bytes accessed | tf_op | source)
XLA Modules:
  0.0 109.7 jit_solution(13271070665066721995)
XLA Ops:
  0.6 106.3 %shard_map.58 = (f32[2,192,128]{2,1,0:T(8,128)}, f32[25,64,128]{2,1,0:T(8,128)}) custom-call(f32[12,24,6400]{2,1,0:T(8,128)} %bitcast.4, f32[60,192]{1,0:T(8,128)} %bitcast.5, f32[60,192]{1,0:T(8,128)} %bitcast.6), custom_call_target="tpu_custom_call" | custom-call | tf_op jit(solution)/shard_map/pallas_call | solution.py:437
  106.9 2.8 %shard_map.59 = (f32[192,192]{1,0:T(8,128)}, f32[192,192]{1,0:T(8,128)}, f32[50,60,60]{2,1,0:T(8,128)}) custom-call(f32[2,192,128]{2,1,0:T(8,128)} %get-tuple-element.8.full, f32[25,64,128]{2,1,0:T(8,128)} %get-tuple-element.9.core), custom_call_target="tpu_custom_call" | custom-call | tf_op jit(solution)/shard_map/pallas_call | solution.py:489
